TPU v7x, 32 devices: a whole 2x2x4 slice. The times are simulated.
32 devices in a mesh: ctx: 8 (over z, core), head: 4 (over y, x).
Axes of the slice: x: 2, y: 2, z: 4, core: 2. Of those that a mesh axis runs over, the one named last changes fastest.
Arguments:
- queries: bfloat16 [12288, 3072], P('ctx', 'head'), may hold values from -160 to 160
- key_states: bfloat16 [12288, 3072], P('ctx', 'head'), may hold values from -12 to 12
- value_states: bfloat16 [12288, 3072], P('ctx', 'head'), may hold values from -18 to 18
- out_grads: bfloat16 [12288, 3072], P(('ctx', 'head')), may hold values from -6 to 6
- pattern: int32 [32, 8], replicated, may hold values from -1 to 31, as said below
Outputs:
- attended: bfloat16 [12288, 3072], P(('ctx', 'head'))
- query_grads: bfloat16 [12288, 3072], P('ctx', 'head')
- key_grads: bfloat16 [12288, 3072], P('ctx', 'head')
- value_grads: bfloat16 [12288, 3072], P('ctx', 'head')
Inputs may be any that keep to these rules, and one draw needn't show every extreme that they name: `pattern`: row t lists distinct tiles whose frame tile (tile // 4) differs from that of t by at most one; t itself is always listed; -1 marks an empty slot and empty slots come last; three or more tiles are listed in every row.
All inputs are finite; a program needn't handle non-finite values.
Results may differ from a plain program's by a relative error of at most 0.035.
Values may be sent and summed in bfloat16 or wider, within the bound.
A program may use at most 320 MiB of HBM per device.

v0:
```python
import math

import jax
import jax.numpy as jnp
from jax import lax
from jax.sharding import PartitionSpec as P

HD = 128
TILE = 384
SPT = 4
KSLOT = 8


def with_halo(block, sides, width):
    for axis, dim in sides:
        count = lax.axis_size(axis)
        forward = [(i, i + 1) for i in range(count - 1)]
        backward = [(target, source) for source, target in forward]
        low = lax.ppermute(
            lax.slice_in_dim(block, block.shape[dim] - width, None, axis=dim), axis, forward
        )
        high = lax.ppermute(lax.slice_in_dim(block, 0, width, axis=dim), axis, backward)
        block = jnp.concatenate([low, block, high], axis=dim)
    return block


def from_behind(block, axis, distance):
    devices = range(lax.axis_size(axis))
    route = [(i - distance, i) for i in devices if i - distance in devices]
    return lax.ppermute(block, axis, route)


def masked_scores(query_tiles, key_sel, allowed):
    score_scale = 1.0 / math.sqrt(HD)
    scores = (
        jnp.einsum("aqd,astd->aqst", query_tiles, key_sel, preferred_element_type=jnp.float32)
        * score_scale
    )
    return jnp.where(allowed[:, None, :, None], scores, -jnp.inf)


def forward_tiles(query_tiles, key_tiles, value_tiles, slot_index, allowed):
    key_sel = jnp.take(key_tiles, slot_index, axis=0)
    value_sel = jnp.take(value_tiles, slot_index, axis=0)
    scores = masked_scores(query_tiles, key_sel, allowed)
    row_max = jnp.max(scores, axis=(2, 3))
    row_total = jnp.sum(jnp.exp(scores - row_max[:, :, None, None]), axis=(2, 3))
    log_total = row_max + jnp.log(row_total)
    weights = jnp.exp(scores - log_total[:, :, None, None]).astype(jnp.bfloat16)
    result = jnp.einsum("aqst,astd->aqd", weights, value_sel, preferred_element_type=jnp.float32)
    return (result.astype(jnp.bfloat16), log_total)


def add_to_tiles(terms, slot_index, allowed, tile_count):
    tile_rows, head_cols = (terms.shape[2], terms.shape[3])
    kept = jnp.where(allowed[:, :, None, None], terms, 0.0)
    flat_terms = kept.reshape(-1, tile_rows, head_cols)
    flat_index = slot_index.reshape(-1)
    return jnp.zeros((tile_count, tile_rows, head_cols), jnp.float32).at[flat_index].add(flat_terms)


def backward_tiles(
    query_tiles, grad_tiles, log_total, delta, key_tiles, value_tiles, slot_index, allowed
):
    score_scale = 1.0 / math.sqrt(HD)
    key_sel = jnp.take(key_tiles, slot_index, axis=0)
    value_sel = jnp.take(value_tiles, slot_index, axis=0)
    scores = masked_scores(query_tiles, key_sel, allowed)
    weights = jnp.exp(scores - log_total[:, :, None, None])
    weights_low = weights.astype(jnp.bfloat16)
    grad_weights = jnp.einsum(
        "aqd,astd->aqst", grad_tiles, value_sel, preferred_element_type=jnp.float32
    )
    grad_scores = (weights * (grad_weights - delta[:, :, None, None])).astype(jnp.bfloat16)
    key_terms = (
        jnp.einsum("aqst,aqd->astd", grad_scores, query_tiles, preferred_element_type=jnp.float32)
        * score_scale
    )
    value_terms = jnp.einsum(
        "aqst,aqd->astd", weights_low, grad_tiles, preferred_element_type=jnp.float32
    )
    tile_count = key_tiles.shape[0]
    key_grad = add_to_tiles(key_terms, slot_index, allowed, tile_count)
    value_grad = add_to_tiles(value_terms, slot_index, allowed, tile_count)
    query_grad = None
    query_grad = (
        jnp.einsum("aqst,astd->aqd", grad_scores, key_sel, preferred_element_type=jnp.float32)
        * score_scale
    )
    return (query_grad, key_grad, value_grad)


def shards(queries, key_states, value_states, out_grads, pattern):
    row_count, col_count = queries.shape
    heads_here = col_count // HD
    rim_rows = SPT * TILE
    own_tiles = row_count // TILE
    frames = own_tiles // SPT
    ext_tiles = own_tiles + 2 * SPT
    first_tile = lax.axis_index("ctx") * own_tiles
    base_tile = first_tile - SPT
    grads_heads = lax.all_to_all(out_grads, "head", split_axis=1, concat_axis=0, tiled=True)
    rims = with_halo(jnp.stack((key_states, value_states)), (("ctx", 1),), rim_rows)
    listed = lax.dynamic_slice_in_dim(pattern, first_tile, own_tiles, 0)
    allowed = listed >= 0
    slot_index = jnp.where(allowed, listed - base_tile, 0)
    index_frames = slot_index.reshape(frames, SPT, KSLOT)
    allowed_frames = allowed.reshape(frames, SPT, KSLOT)
    outputs, totals, deltas, query_parts, key_parts, value_parts = ([], [], [], [], [], [])
    for head_num in range(heads_here):
        head_cols = slice(head_num * HD, (head_num + 1) * HD)
        query_tiles = queries[:, head_cols].reshape(frames, SPT, TILE, HD)
        grad_tiles = grads_heads[:, head_cols].reshape(frames, SPT, TILE, HD)
        key_tiles = rims[0, :, head_cols].reshape(ext_tiles, TILE, HD)
        value_tiles = rims[1, :, head_cols].reshape(ext_tiles, TILE, HD)

        def forward_frame(frame_items):
            return forward_tiles(
                frame_items[0], key_tiles, value_tiles, frame_items[1], frame_items[2]
            )

        head_out, log_total = lax.map(forward_frame, (query_tiles, index_frames, allowed_frames))
        delta = jnp.sum(grad_tiles.astype(jnp.float32) * head_out.astype(jnp.float32), axis=-1)

        def backward_frame(grad_sums, frame_items):
            query_grad, key_grad, value_grad = backward_tiles(
                frame_items[0],
                frame_items[1],
                frame_items[2],
                frame_items[3],
                key_tiles,
                value_tiles,
                frame_items[4],
                frame_items[5],
            )
            return (
                (grad_sums[0] + key_grad, grad_sums[1] + value_grad),
                query_grad.astype(jnp.bfloat16),
            )

        zero_grads = jnp.zeros((ext_tiles, TILE, HD), jnp.float32)
        (key_grad, value_grad), query_grad = lax.scan(
            backward_frame,
            (zero_grads, zero_grads),
            (query_tiles, grad_tiles, log_total, delta, index_frames, allowed_frames),
        )
        outputs.append(head_out.reshape(row_count, HD))
        totals.append(log_total.reshape(row_count))
        deltas.append(delta.reshape(row_count))
        query_parts.append(query_grad.reshape(row_count, HD))
        key_parts.append(key_grad)
        value_parts.append(value_grad)
    attended = lax.all_to_all(
        jnp.concatenate(outputs, axis=1), "head", split_axis=0, concat_axis=1, tiled=True
    )
    grad_parts = jnp.stack((jnp.stack(key_parts), jnp.stack(value_parts)))
    own_part = grad_parts[:, :, SPT : SPT + own_tiles]
    lower_part = grad_parts[:, :, :SPT]
    upper_part = grad_parts[:, :, SPT + own_tiles :]
    from_above = from_behind(lower_part.astype(jnp.bfloat16), "ctx", -1).astype(lower_part.dtype)
    from_below = from_behind(upper_part, "ctx", 1)
    zero_rim = jnp.zeros((2, heads_here, own_tiles - SPT, TILE, HD), jnp.float32)
    own_part = (
        own_part
        + jnp.concatenate((from_below, zero_rim), axis=2)
        + jnp.concatenate((zero_rim, from_above), axis=2)
    )
    grads_out = (
        own_part.transpose(0, 2, 3, 1, 4).reshape(2, row_count, col_count).astype(jnp.bfloat16)
    )
    return (attended, jnp.concatenate(query_parts, axis=1), grads_out[0], grads_out[1])


def solution(mesh):
    return jax.shard_map(
        shards,
        mesh=mesh,
        in_specs=(
            P("ctx", "head"),
            P("ctx", "head"),
            P("ctx", "head"),
            P(("ctx", "head"), None),
            P(),
        ),
        out_specs=(P(("ctx", "head"), None), P("ctx", "head"), P("ctx", "head"), P("ctx", "head")),
        check_vma=False,
    )
```

profile of v0, /device:TPU:1, one launch (start us, length us, event | category | flops | bytes accessed | tf_op | source)
XLA Modules:
  0.0 742.6 jit_solution(141597660512651505)
XLA Ops:
  0.6 5.1 pad_maximum_fusion.2
  7.9 4.6 collective-permute-start
  22.8 22.8 %all-to-all-done.1 = bf16[384,4,768]{0,2,1:T(8,128)(2,1)S(1)} async-done(((bf16[384,4,768]{0,2,1:T(8,128)(2,1)}), bf16[384,4,768]{0,2,1:T(8,128)(2,1)S(1)}, u32[]{:S(2)}, u32[]{:S(2)}) %all-to-all-start.1) | async-done | bytes 2359328 | tf_op jit(solution)/shard_map/all_to_all | solution.py:102
  47.0 4.4 copy.177
  63.8 6.9 pad_maximum_fusion
  70.7 4.7 fusion.170
  83.0 3.9 gather_fusion.10
  86.9 4.0 gather_fusion.4
  94.7 3.9 gather_fusion.8
  102.5 3.9 gather_fusion.3
  118.2 11.2 %fusion.38 = f32[4,8,384,384]{3,2,1,0:T(8,128)} fusion(bf16[4,384,128,1]{2,1,3,0:T(8,128)(2,1)S(1)} %bitcast.466, bf16[4,8,384,128]{3,2,1,0:T(8,128)(2,1)} %bitcast.434, pred[4,8]{1,0:T(4,128)(4,1)S(1)} %copy.140), kind=kOutput, calls=%fused_computation.123 | convolution fusion | flops 1209532416 | bytes 22413344 | tf_op jit(solution)/shard_map/while/body/eval_jaxpr/aqd,astd->aqst/dot_general | solution.py:36
  129.4 8.1 %fusion.44 = f32[4,8,384,384]{3,2,1,0:T(8,128)} fusion(bf16[4,384,128,1]{2,1,3,0:T(8,128)(2,1)S(1)} %bitcast.464, bf16[4,8,384,128]{3,2,1,0:T(8,128)(2,1)S(1)} %bitcast.432, pred[4,8]{1,0:T(4,128)(4,1)S(1)} %copy.140), kind=kOutput, calls=%fused_computation.129 | convolution fusion | flops 1209532416 | bytes 22413344 | tf_op jit(solution)/shard_map/while/body/eval_jaxpr/aqd,astd->aqst/dot_general | solution.py:36
  137.5 7.8 %fusion.47 = f32[4,8,384,384]{3,2,1,0:T(8,128)} fusion(bf16[4,384,128,1]{2,1,3,0:T(8,128)(2,1)S(1)} %bitcast.463, bf16[4,8,384,128]{3,2,1,0:T(8,128)(2,1)S(1)} %bitcast.430, pred[4,8]{1,0:T(4,128)(4,1)S(1)} %copy.140), kind=kOutput, calls=%fused_computation.132 | convolution fusion | flops 1209532416 | bytes 22413344 | tf_op jit(solution)/shard_map/while/body/eval_jaxpr/aqd,astd->aqst/dot_general | solution.py:36
  145.4 8.0 %fusion.50 = f32[4,8,384,384]{3,2,1,0:T(8,128)} fusion(bf16[4,384,128,1]{2,1,3,0:T(8,128)(2,1)S(1)} %bitcast.460, bf16[4,8,384,128]{3,2,1,0:T(8,128)(2,1)S(1)} %bitcast.428, pred[4,8]{1,0:T(4,128)(4,1)S(1)} %copy.140), kind=kOutput, calls=%fused_computation.135 | convolution fusion | flops 1209532416 | bytes 22413344 | tf_op jit(solution)/shard_map/while/body/eval_jaxpr/aqd,astd->aqst/dot_general | solution.py:36
  153.3 13.3 %bitcast_reduce_fusion = (f32[4,384]{1,0:T(4,128)}, f32[4,384]{1,0:T(4,128)}, f32[4,8,384,384]{3,2,1,0:T(8,128)}) fusion(pred[4,8]{1,0:T(4,128)(4,1)S(1)} %copy.139, f32[4,8,384,384]{3,2,1,0:T(8,128)} %fusion.38, bf16[4,384,128,1]{2,1,3,0:T(8,128)(2,1)S(1)} %bitcast.458, bf16[4,8,384,128]{3,2,1,0:T(8,128)(2,1)S(1)} %bitcast.424, pred[4,8]{1,0:T(4,128)(4,1)S(1)} %copy.140), kind=kOutput, calls=%fused_computation.42 | convolution fusion | flops 1237840896 | bytes 41300032 | tf_op jit(solution)/shard_map/while/body/eval_jaxpr/aqd,astd->aqst/dot_general | solution.py:36
  166.6 39.9 %fusion.7 = (f32[4,384]{1,0:T(4,128)}, f32[4,384]{1,0:T(4,128)}, f32[4,384]{1,0:T(4,128)}, f32[4,384]{1,0:T(4,128)S(1)}, f32[4,384]{1,0:T(4,128)}, /*index=5*/f32[4,384]{1,0:T(4,128)}, f32[4,8,384,384]{3,2,1,0:T(8,128)}) fusion(f32[4,8,384,384]{3,2,1,0:T(8,128)} %get-tuple-element.354, f32[4,384]{1,0:T(4,128)} %get-tuple-element.279, ...), kind=kOutput, calls=%fused_computation.44 | convolution fusion | flops 1303895040 | bytes 116834368 | tf_op jit(solution)/shard_map/while/body/eval_jaxpr/aqd,astd->aqst/dot_general | solution.py:36
  207.9 10.8 %constant_dynamic-update-slice_fusion.5 = (bf16[4,384,768]{1,2,0:T(8,128)(2,1)}, bf16[4,384,128]{1,2,0:T(8,128)(2,1)S(1)}) fusion(bf16[4,8,384,128]{3,2,1,0:T(8,128)(2,1)} %bitcast.480, pred[4,8]{1,0:T(4,128)(4,1)S(1)} %copy.140, f32[4,8,384,384]{3,2,1,0:T(8,128)} %fusion.38, f32[4,384]{1,0:T(4,128)S(1)} %get-tuple-element.381, pred[4,8]{1,0:T(4,128)(4,1)S(1)} %copy.139), kind=kOutput, calls=%fused_computation.219 | convolution fusion | flops 1228603392 | bytes 22812736 | tf_op jit(solution)/shard_map/while/body/eval_jaxpr/aqst,astd->aqd/dot_general | solution.py:50
  218.7 10.3 %broadcast_select_fusion.5 = f32[4,8,384,128]{3,2,1,0:T(8,128)} fusion(pred[4,8]{1,0:T(4,128)(4,1)S(1)} %copy.139, bf16[4,384,128,1]{2,1,3,0:T(8,128)(2,1)S(1)} %bitcast.500, f32[4,8,384,384]{3,2,1,0:T(8,128)} %fusion.38, f32[4,384]{1,0:T(4,128)S(1)} %get-tuple-element.381), kind=kOutput, calls=%fused_computation.109 | convolution fusion | flops 1228406784 | bytes 25565216 | tf_op jit(solution)/shard_map/while/body/eval_jaxpr/aqst,aqd->astd/dot_general | solution.py:79
  229.1 11.3 %fusion.5 = bf16[4,384,8,384]{1,3,2,0:T(8,128)(2,1)} fusion(f32[4,8,384,384]{3,2,1,0:T(8,128)} %fusion.38, f32[4,384]{1,0:T(4,128)S(1)} %multiply_reduce_fusion.5, f32[4,384]{1,0:T(4,128)S(1)} %get-tuple-element.381, pred[4,8]{1,0:T(4,128)(4,1)S(1)} %copy.139, bf16[4,384,128,1]{2,1,3,0:T(8,128)(2,1)S(1)} %bitcast.501, ...), kind=kOutput, calls=%fused_computation.39 | convolution fusion | flops 1237843968 | bytes 31862848 | tf_op jit(solution)/shard_map/while/body/eval_jaxpr/aqd,astd->aqst/dot_general | solution.py:71
  240.4 27.8 %fusion.10 = (f32[4,384]{1,0:T(4,128)S(1)}, f32[4,384]{1,0:T(4,128)S(1)}, f32[4,384]{1,0:T(4,128)S(1)}, f32[4,384]{1,0:T(4,128)S(1)}) fusion(f32[4,8,384,384]{3,2,1,0:T(8,128)} %fusion.50, f32[4,384]{1,0:T(4,128)S(1)} %copy-done.41, pred[4,8]{1,0:T(4,128)(4,1)S(1)} %copy.139, f32[4,384]{1,0:T(4,128)S(1)} %copy-done.42, ...), kind=kLoop, calls=%fused_computation.50 | loop fusion | flops 75491328 | bytes 75546656 | tf_op jit(solution)/shard_map/while/body/eval_jaxpr/reduce_sum | solution.py:47
  268.3 6.2 broadcast_select_fusion.4
  274.5 7.0 constant_dynamic-update-slice_fusion.4
  281.6 15.4 %fusion.4 = bf16[4,384,8,384]{1,3,2,0:T(8,128)(2,1)} fusion(f32[4,8,384,384]{3,2,1,0:T(8,128)} %get-tuple-element.355, f32[4,384]{1,0:T(4,128)S(1)} %multiply_reduce_fusion.4, f32[4,384]{1,0:T(4,128)S(1)} %get-tuple-element.385, pred[4,8]{1,0:T(4,128)(4,1)S(1)} %copy.139, bf16[4,384,128,1]{2,1,3,0:T(8,128)(2,1)S(1)} %bitcast.498, ...), kind=kOutput, calls=%fused_computation.37 | convolution fusion | flops 1237843968 | bytes 31862848 | tf_op jit(solution)/shard_map/while/body/eval_jaxpr/aqd,astd->aqst/dot_general | solution.py:71
  297.1 10.3 %broadcast_select_fusion.3 = f32[4,8,384,128]{3,2,1,0:T(8,128)} fusion(pred[4,8]{1,0:T(4,128)(4,1)S(1)} %copy.139, bf16[4,384,128,1]{2,1,3,0:T(8,128)(2,1)S(1)} %bitcast.494, f32[4,8,384,384]{3,2,1,0:T(8,128)} %fusion.44, f32[4,384]{1,0:T(4,128)S(1)} %get-tuple-element.384), kind=kOutput, calls=%fused_computation.107 | convolution fusion | flops 1228406784 | bytes 25565216 | tf_op jit(solution)/shard_map/while/body/eval_jaxpr/aqst,aqd->astd/dot_general | solution.py:79
  307.8 7.0 constant_dynamic-update-slice_fusion.3
  314.9 15.6 %fusion.3 = bf16[4,384,8,384]{1,3,2,0:T(8,128)(2,1)} fusion(f32[4,8,384,384]{3,2,1,0:T(8,128)} %fusion.44, f32[4,384]{1,0:T(4,128)S(1)} %multiply_reduce_fusion.3, f32[4,384]{1,0:T(4,128)S(1)} %get-tuple-element.384, pred[4,8]{1,0:T(4,128)(4,1)S(1)} %copy.139, bf16[4,384,128,1]{2,1,3,0:T(8,128)(2,1)S(1)} %bitcast.495, ...), kind=kOutput, calls=%fused_computation.35 | convolution fusion | flops 1237843968 | bytes 31862848 | tf_op jit(solution)/shard_map/while/body/eval_jaxpr/aqd,astd->aqst/dot_general | solution.py:71
  330.6 10.3 %broadcast_select_fusion.2 = f32[4,8,384,128]{3,2,1,0:T(8,128)} fusion(pred[4,8]{1,0:T(4,128)(4,1)S(1)} %copy.139, bf16[4,384,128,1]{2,1,3,0:T(8,128)(2,1)S(1)} %bitcast.491, f32[4,8,384,384]{3,2,1,0:T(8,128)} %fusion.47, f32[4,384]{1,0:T(4,128)S(1)} %get-tuple-element.383), kind=kOutput, calls=%fused_computation.106 | convolution fusion | flops 1228406784 | bytes 25565216 | tf_op jit(solution)/shard_map/while/body/eval_jaxpr/aqst,aqd->astd/dot_general | solution.py:79
  341.3 7.0 constant_dynamic-update-slice_fusion.2
  348.4 15.4 %fusion.2 = bf16[4,384,8,384]{1,3,2,0:T(8,128)(2,1)} fusion(f32[4,8,384,384]{3,2,1,0:T(8,128)} %fusion.47, f32[4,384]{1,0:T(4,128)S(1)} %multiply_reduce_fusion.2, f32[4,384]{1,0:T(4,128)S(1)} %get-tuple-element.383, pred[4,8]{1,0:T(4,128)(4,1)S(1)} %copy.139, bf16[4,384,128,1]{2,1,3,0:T(8,128)(2,1)S(1)} %bitcast.492, ...), kind=kOutput, calls=%fused_computation.33 | convolution fusion | flops 1237843968 | bytes 31862848 | tf_op jit(solution)/shard_map/while/body/eval_jaxpr/aqd,astd->aqst/dot_general | solution.py:71
  363.9 10.3 %broadcast_select_fusion.1 = f32[4,8,384,128]{3,2,1,0:T(8,128)} fusion(pred[4,8]{1,0:T(4,128)(4,1)S(1)} %copy.139, bf16[4,384,128,1]{2,1,3,0:T(8,128)(2,1)S(1)} %bitcast.488, f32[4,8,384,384]{3,2,1,0:T(8,128)} %fusion.50, f32[4,384]{1,0:T(4,128)S(1)} %get-tuple-element.382), kind=kOutput, calls=%fused_computation.105 | convolution fusion | flops 1228406784 | bytes 25565216 | tf_op jit(solution)/shard_map/while/body/eval_jaxpr/aqst,aqd->astd/dot_general | solution.py:79
  374.6 7.3 constant_dynamic-update-slice_fusion.1
  382.1 15.5 %fusion.1 = bf16[4,384,8,384]{1,3,2,0:T(8,128)(2,1)} fusion(f32[4,8,384,384]{3,2,1,0:T(8,128)} %fusion.50, f32[4,384]{1,0:T(4,128)S(1)} %multiply_reduce_fusion.1, f32[4,384]{1,0:T(4,128)S(1)} %get-tuple-element.382, pred[4,8]{1,0:T(4,128)(4,1)S(1)} %copy.139, bf16[4,384,128,1]{2,1,3,0:T(8,128)(2,1)S(1)} %bitcast.489, ...), kind=kOutput, calls=%fused_computation.31 | convolution fusion | flops 1237843968 | bytes 31862848 | tf_op jit(solution)/shard_map/while/body/eval_jaxpr/aqd,astd->aqst/dot_general | solution.py:71
  397.6 10.3 %broadcast_select_fusion = f32[4,8,384,128]{3,2,1,0:T(8,128)} fusion(pred[4,8]{1,0:T(4,128)(4,1)S(1)} %copy.139, bf16[4,384,128,1]{2,1,3,0:T(8,128)(2,1)S(1)} %bitcast.485, f32[4,8,384,384]{3,2,1,0:T(8,128)} %get-tuple-element.354, f32[4,384]{1,0:T(4,128)S(1)} %copy-done.44), kind=kOutput, calls=%fused_computation.104 | convolution fusion | flops 1228406784 | bytes 25565216 | tf_op jit(solution)/shard_map/while/body/eval_jaxpr/aqst,aqd->astd/dot_general | solution.py:79
  408.3 7.0 constant_dynamic-update-slice_fusion
  415.4 14.4 %fusion = bf16[4,384,8,384]{1,3,2,0:T(8,128)(2,1)} fusion(f32[4,8,384,384]{3,2,1,0:T(8,128)} %get-tuple-element.354, f32[4,384]{1,0:T(4,128)S(1)} %multiply_reduce_fusion, f32[4,384]{1,0:T(4,128)S(1)} %copy-done.44, pred[4,8]{1,0:T(4,128)(4,1)S(1)} %copy.139, bf16[4,384,128,1]{2,1,3,0:T(8,128)(2,1)S(1)} %bitcast.486, ...), kind=kOutput, calls=%fused_computation.29 | convolution fusion | flops 1237843968 | bytes 31862848 | tf_op jit(solution)/shard_map/while/body/eval_jaxpr/aqd,astd->aqst/dot_general | solution.py:71
  430.0 10.2 %scatter_fusion.6 = f32[12,384,128]{2,1,0:T(8,128)S(1)} fusion(f32[12,384,128]{2,1,0:T(8,128)S(1)} %broadcast.164.clone, s32[32]{0:T(128)S(1)} %copy-done.40, f32[32,384,128]{2,1,0:T(8,128)} %bitcast.453), kind=kCustom, calls=%fused_computation.18 | custom fusion | flops 1572864 | bytes 18874496 | tf_op jit(solution)/shard_map/while/body/eval_jaxpr/scatter-add | solution.py:59
  441.8 8.9 %multiply_select_fusion.11 = f32[4,8,384,128]{3,2,1,0:T(8,128)} fusion(pred[4,8]{1,0:T(4,128)(4,1)S(1)} %copy.139, bf16[4,384,8,384]{1,3,2,0:T(8,128)(2,1)} %fusion.5, bf16[4,384,128,1]{2,1,3,0:T(8,128)(2,1)S(1)} %bitcast.467), kind=kOutput, calls=%fused_computation.101 | convolution fusion | flops 1211105280 | bytes 16121888 | tf_op jit(solution)/shard_map/while/body/eval_jaxpr/aqst,aqd->astd/dot_general | solution.py:76
  451.0 10.1 %scatter_fusion = f32[12,384,128]{2,1,0:T(8,128)S(1)} fusion(f32[12,384,128]{2,1,0:T(8,128)S(1)} %broadcast.164.clone.6, s32[32]{0:T(128)S(1)} %copy-done.40, f32[32,384,128]{2,1,0:T(8,128)} %bitcast.407), kind=kCustom, calls=%fused_computation.12 | custom fusion | flops 1572864 | bytes 18874496 | tf_op jit(solution)/shard_map/while/body/eval_jaxpr/scatter-add | solution.py:59
  462.7 9.4 %multiply_select_fusion.10 = f32[4,8,384,128]{3,2,1,0:T(8,128)} fusion(pred[4,8]{1,0:T(4,128)(4,1)S(1)} %copy.139, bf16[4,384,8,384]{1,3,2,0:T(8,128)(2,1)} %fusion.4, bf16[4,384,128,1]{2,1,3,0:T(8,128)(2,1)S(1)} %bitcast.503), kind=kOutput, calls=%fused_computation.100 | convolution fusion | flops 1211105280 | bytes 16121888 | tf_op jit(solution)/shard_map/while/body/eval_jaxpr/aqst,aqd->astd/dot_general | solution.py:76
  472.1 4.6 multiply_select_fusion.9
  476.8 5.9 multiply_select_fusion.8
  482.8 4.5 multiply_select_fusion.7
  487.3 4.9 multiply_select_fusion.6
  492.4 10.1 %scatter_fusion.7 = f32[12,384,128]{2,1,0:T(8,128)S(1)} fusion(f32[12,384,128]{2,1,0:T(8,128)S(1)} %broadcast.164.clone.1, s32[32]{0:T(128)S(1)} %copy-done.40, f32[32,384,128]{2,1,0:T(8,128)} %bitcast.452), kind=kCustom, calls=%fused_computation.19 | custom fusion | flops 1572864 | bytes 18874496 | tf_op jit(solution)/shard_map/while/body/eval_jaxpr/scatter-add | solution.py:59
  504.2 10.1 %scatter_fusion.8 = f32[12,384,128]{2,1,0:T(8,128)S(1)} fusion(f32[12,384,128]{2,1,0:T(8,128)S(1)} %broadcast.164.clone.2, s32[32]{0:T(128)S(1)} %copy-done.40, f32[32,384,128]{2,1,0:T(8,128)} %bitcast.454), kind=kCustom, calls=%fused_computation.20 | custom fusion | flops 1572864 | bytes 18874496 | tf_op jit(solution)/shard_map/while/body/eval_jaxpr/scatter-add | solution.py:59
  516.1 10.1 %scatter_fusion.9 = f32[12,384,128]{2,1,0:T(8,128)S(1)} fusion(f32[12,384,128]{2,1,0:T(8,128)S(1)} %broadcast.164.clone.3, s32[32]{0:T(128)S(1)} %copy-done.40, f32[32,384,128]{2,1,0:T(8,128)} %bitcast.455), kind=kCustom, calls=%fused_computation.21 | custom fusion | flops 1572864 | bytes 18874496 | tf_op jit(solution)/shard_map/while/body/eval_jaxpr/scatter-add | solution.py:59
  528.0 10.1 %scatter_fusion.10 = f32[12,384,128]{2,1,0:T(8,128)S(1)} fusion(f32[12,384,128]{2,1,0:T(8,128)S(1)} %broadcast.164.clone.4, s32[32]{0:T(128)S(1)} %copy-done.40, f32[32,384,128]{2,1,0:T(8,128)} %bitcast.456), kind=kCustom, calls=%fused_computation.22 | custom fusion | flops 1572864 | bytes 18874496 | tf_op jit(solution)/shard_map/while/body/eval_jaxpr/scatter-add | solution.py:59
  539.9 10.1 %scatter_fusion.11 = f32[12,384,128]{2,1,0:T(8,128)S(1)} fusion(f32[12,384,128]{2,1,0:T(8,128)S(1)} %broadcast.164.clone.5, s32[32]{0:T(128)S(1)} %copy-done.40, f32[32,384,128]{2,1,0:T(8,128)} %bitcast.457), kind=kCustom, calls=%fused_computation.23 | custom fusion | flops 1572864 | bytes 18874496 | tf_op jit(solution)/shard_map/while/body/eval_jaxpr/scatter-add | solution.py:59
  551.7 10.1 %scatter_fusion.1 = f32[12,384,128]{2,1,0:T(8,128)S(1)} fusion(f32[12,384,128]{2,1,0:T(8,128)S(1)} %broadcast.164.clone.7, s32[32]{0:T(128)S(1)} %copy-done.40, f32[32,384,128]{2,1,0:T(8,128)} %bitcast.406), kind=kCustom, calls=%fused_computation.13 | custom fusion | flops 1572864 | bytes 18874496 | tf_op jit(solution)/shard_map/while/body/eval_jaxpr/scatter-add | solution.py:59
  563.6 10.1 %scatter_fusion.2 = f32[12,384,128]{2,1,0:T(8,128)S(1)} fusion(f32[12,384,128]{2,1,0:T(8,128)S(1)} %broadcast.164.clone.8, s32[32]{0:T(128)S(1)} %copy-done.40, f32[32,384,128]{2,1,0:T(8,128)} %bitcast.405), kind=kCustom, calls=%fused_computation.14 | custom fusion | flops 1572864 | bytes 18874496 | tf_op jit(solution)/shard_map/while/body/eval_jaxpr/scatter-add | solution.py:59
  575.4 10.1 %scatter_fusion.3 = f32[12,384,128]{2,1,0:T(8,128)S(1)} fusion(f32[12,384,128]{2,1,0:T(8,128)S(1)} %broadcast.164.clone.9, s32[32]{0:T(128)S(1)} %copy-done.40, f32[32,384,128]{2,1,0:T(8,128)} %bitcast.404), kind=kCustom, calls=%fused_computation.15 | custom fusion | flops 1572864 | bytes 18874496 | tf_op jit(solution)/shard_map/while/body/eval_jaxpr/scatter-add | solution.py:59
  587.3 10.1 %scatter_fusion.4 = f32[12,384,128]{2,1,0:T(8,128)S(1)} fusion(f32[12,384,128]{2,1,0:T(8,128)S(1)} %broadcast.164.clone.10, s32[32]{0:T(128)S(1)} %copy-done.40, f32[32,384,128]{2,1,0:T(8,128)} %bitcast.403), kind=kCustom, calls=%fused_computation.16 | custom fusion | flops 1572864 | bytes 18874496 | tf_op jit(solution)/shard_map/while/body/eval_jaxpr/scatter-add | solution.py:59
  599.1 10.1 %scatter_fusion.5 = f32[12,384,128]{2,1,0:T(8,128)S(1)} fusion(f32[12,384,128]{2,1,0:T(8,128)S(1)} %broadcast.164.clone.11, s32[32]{0:T(128)S(1)} %copy-done.40, f32[32,384,128]{2,1,0:T(8,128)} %bitcast.402), kind=kCustom, calls=%fused_computation.17 | custom fusion | flops 1572864 | bytes 18874496 | tf_op jit(solution)/shard_map/while/body/eval_jaxpr/scatter-add | solution.py:59
  610.8 8.5 %fusion.30 = f32[2,6,4,384,128]{4,3,2,1,0:T(8,128)} fusion(f32[1,6,12,384,128]{4,3,2,1,0:T(8,128)} %bitcast.390, f32[1,6,12,384,128]{4,3,2,1,0:T(8,128)} %bitcast.393), kind=kLoop, calls=%fused_computation.89 | loop fusion | flops 2359296 | bytes 37748736 | tf_op jit(solution)/shard_map/stack | solution.py:156
  619.3 4.6 collective-permute-start.2
  627.6 6.9 fusion.35
  638.0 7.2 fusion.102
  645.2 8.1 %fusion.101 = bf16[4,384,128]{2,1,0:T(8,128)(2,1)S(1)} fusion(bf16[4,384,8,384]{1,3,2,0:T(8,128)(2,1)} %fusion.4, bf16[4,8,384,128]{3,2,1,0:T(8,128)(2,1)} %bitcast.468, pred[4,8]{1,0:T(4,128)(4,1)S(1)} %copy.140), kind=kOutput, calls=%fused_computation.200 | convolution fusion | flops 1209925632 | bytes 12976160 | tf_op jit(solution)/shard_map/while/body/eval_jaxpr/aqst,astd->aqd/dot_general | solution.py:87
  654.9 7.3 fusion.100
  662.2 7.5 %fusion.99 = bf16[4,384,128]{2,1,0:T(8,128)(2,1)S(1)} fusion(bf16[4,384,8,384]{1,3,2,0:T(8,128)(2,1)} %fusion.2, bf16[4,8,384,128]{3,2,1,0:T(8,128)(2,1)S(1)} %bitcast.431, pred[4,8]{1,0:T(4,128)(4,1)S(1)} %copy.140), kind=kOutput, calls=%fused_computation.198 | convolution fusion | flops 1209925632 | bytes 12976160 | tf_op jit(solution)/shard_map/while/body/eval_jaxpr/aqst,astd->aqd/dot_general | solution.py:87
  669.8 7.3 fusion.98
  679.4 7.2 fusion.97
  690.3 35.6 %collective-permute-done.2 = f32[2,6,4,384,128]{4,3,2,1,0:T(8,128)} collective-permute-done((f32[2,6,4,384,128]{4,3,2,1,0:T(8,128)}, f32[2,6,4,384,128]{4,3,2,1,0:T(8,128)}, u32[]{:S(2)}, u32[]{:S(2)}) %collective-permute-start.2) | collective-permute-done | bytes 9437216 | tf_op jit(solution)/shard_map/ppermute | solution.py:30
  725.9 8.5 %fusion.36 = bf16[2,4,384,6,128]{4,2,1,3,0:T(8,128)(2,1)S(1)} fusion(bf16[2,6,4,384,128]{4,3,2,1,0:T(8,128)(2,1)} %collective-permute-done.3, f32[2,6,4,384,128]{4,3,2,1,0:T(8,128)} %collective-permute-done.2, f32[1,6,12,384,128]{4,3,2,1,0:T(8,128)} %bitcast.395, f32[1,6,12,384,128]{4,3,2,1,0:T(8,128)} %bitcast.392), kind=kLoop, calls=%fused_computation.103 | loop fusion | flops 11796480 | bytes 47185920 | tf_op jit(solution)/shard_map/convert_element_type | solution.py:169
  (255 shorter events, 101.2 us)
Async XLA Ops:
  0.6 11.8 %copy-start.22 = (bf16[384,3072]{1,0:T(8,128)(2,1)S(1)}, bf16[384,3072]{1,0:T(8,128)(2,1)}, u32[]{:S(2)}) copy-start(bf16[384,3072]{1,0:T(8,128)(2,1)} %param.10) | copy-start | bytes 7077892
  5.8 12.7 %copy-start.45 = (s32[32,8]{0,1:T(8,128)S(1)}, s32[32,8]{0,1:T(8,128)}, u32[]{:S(2)}) copy-start(s32[32,8]{0,1:T(8,128)} %param.11) | copy-start | bytes 3076
  5.8 57.3 %collective-permute-start.1 = (bf16[2,1536,768]{2,1,0:T(8,128)(2,1)}, bf16[2,1536,768]{2,1,0:T(8,128)(2,1)}, u32[]{:S(2)}, u32[]{:S(2)}) collective-permute-start(bf16[2,1536,768]{2,1,0:T(8,128)(2,1)} %pad_maximum_fusion.2), channel_id=1, source_target_pairs={{4,0},{8,4},{12,8},{16,12},{20,16},{24,20},{28,24},{5,1},{9,5},{13... | collective-permute-start | bytes 14155784 | tf_op jit(solution)/shard_map/ppermute | solution.py:22
  7.9 55.9 %collective-permute-start = (bf16[2,1536,768]{2,1,0:T(8,128)(2,1)}, bf16[2,1536,768]{2,1,0:T(8,128)(2,1)}, u32[]{:S(2)}, u32[]{:S(2)}) collective-permute-start(bf16[2,1536,768]{2,1,0:T(8,128)(2,1)} %pad_maximum_fusion.2), channel_id=1, source_target_pairs={{0,4},{4,8},{8,12},{12,16},{16,20},{20,24},{24,28},{1,5},{5,9},{9,... | collective-permute-start | bytes 14155784 | tf_op jit(solution)/shard_map/ppermute | solution.py:19
  14.9 30.7 %all-to-all-start.1 = ((bf16[384,4,768]{0,2,1:T(8,128)(2,1)}), bf16[384,4,768]{0,2,1:T(8,128)(2,1)S(1)}, u32[]{:S(2)}, u32[]{:S(2)}) async-start(bf16[384,4,768]{0,2,1:T(8,128)(2,1)} %bitcast.449), calls=%async_computation.1 | async-start | bytes 4718592 | tf_op jit(solution)/shard_map/all_to_all | solution.py:102
  47.0 16.8 %copy-start.9 = (bf16[1536,768]{1,0:T(8,128)(2,1)S(1)}, bf16[1536,768]{1,0:T(8,128)(2,1)}, u32[]{:S(2)}) copy-start(bf16[1536,768]{1,0:T(8,128)(2,1)} %param.9) | copy-start | bytes 7077892
  54.1 9.6 %copy-start.26 = (bf16[1536,128]{1,0:T(8,128)(2,1)}, bf16[1536,128]{1,0:T(8,128)(2,1)S(1)}, u32[]{:S(2)}) copy-start(bf16[1536,128]{1,0:T(8,128)(2,1)S(1)} %get-tuple-element.327) | copy-start | bytes 1179652
  54.1 9.6 %copy-start.29 = (bf16[1536,128]{1,0:T(8,128)(2,1)}, bf16[1536,128]{1,0:T(8,128)(2,1)S(1)}, u32[]{:S(2)}) copy-start(bf16[1536,128]{1,0:T(8,128)(2,1)S(1)} %get-tuple-element.336) | copy-start | bytes 1179652
  118.2 11.2 %copy-start.6 = (bf16[32,384,128]{2,1,0:T(8,128)(2,1)S(1)}, bf16[32,384,128]{2,1,0:T(8,128)(2,1)}, u32[]{:S(2)}) copy-start(bf16[32,384,128]{2,1,0:T(8,128)(2,1)} %gather_fusion.4) | copy-start | bytes 9437188
  118.2 11.2 %copy-start.16 = (bf16[1536,128]{1,0:T(8,128)(2,1)S(1)}, bf16[1536,128]{1,0:T(8,128)(2,1)}, u32[]{:S(2)}) copy-start(bf16[1536,128]{1,0:T(8,128)(2,1)} %get-tuple-element.342) | copy-start | bytes 1179652
  153.3 13.3 %copy-start.20 = (bf16[32,384,128]{2,1,0:T(8,128)(2,1)S(1)}, bf16[32,384,128]{2,1,0:T(8,128)(2,1)}, u32[]{:S(2)}) copy-start(bf16[32,384,128]{2,1,0:T(8,128)(2,1)} %gather_fusion.2) | copy-start | bytes 9437188
  153.3 13.3 %copy-start.38 = (bf16[1536,128]{1,0:T(8,128)(2,1)S(1)}, bf16[1536,128]{1,0:T(8,128)(2,1)}, u32[]{:S(2)}) copy-start(bf16[1536,128]{1,0:T(8,128)(2,1)} %get-tuple-element.343) | copy-start | bytes 1179652
  207.9 10.8 %copy-start.36 = (bf16[1536,128]{1,0:T(8,128)(2,1)S(1)}, bf16[1536,128]{1,0:T(8,128)(2,1)}, u32[]{:S(2)}) copy-start(bf16[1536,128]{1,0:T(8,128)(2,1)} %get-tuple-element.339) | copy-start | bytes 1179652
  218.6 10.3 %copy-start.37 = (bf16[4,384,128]{1,2,0:T(8,128)(2,1)S(1)}, bf16[4,384,128]{1,2,0:T(8,128)(2,1)}, u32[]{:S(2)}) copy-start(bf16[4,384,128]{1,2,0:T(8,128)(2,1)} %copy.178) | copy-start | bytes 1179652
  218.6 10.4 %copy-start.21 = (bf16[32,384,128]{2,1,0:T(8,128)(2,1)S(1)}, bf16[32,384,128]{2,1,0:T(8,128)(2,1)}, u32[]{:S(2)}) copy-start(bf16[32,384,128]{2,1,0:T(8,128)(2,1)} %gather_fusion.1) | copy-start | bytes 9437188
  229.1 11.3 %copy-start.41 = (f32[4,384]{1,0:T(4,128)S(1)}, f32[4,384]{1,0:T(4,128)}, u32[]{:S(2)}) copy-start(f32[4,384]{1,0:T(4,128)} %get-tuple-element.277) | copy-start | bytes 18436
  229.1 11.3 %copy-start.42 = (f32[4,384]{1,0:T(4,128)S(1)}, f32[4,384]{1,0:T(4,128)}, u32[]{:S(2)}) copy-start(f32[4,384]{1,0:T(4,128)} %get-tuple-element.274) | copy-start | bytes 18436
  229.1 11.3 %copy-start.43 = (f32[4,384]{1,0:T(4,128)S(1)}, f32[4,384]{1,0:T(4,128)}, u32[]{:S(2)}) copy-start(f32[4,384]{1,0:T(4,128)} %get-tuple-element.275) | copy-start | bytes 18436
  229.1 39.1 %slice-start.20 = ((s8[18874368]{0:T(1024)(128)(4,1)}), s8[2097152]{0:T(1024)(128)(4,1)S(1)}, s32[]{:S(2)}) async-start(s8[18874368]{0:T(1024)(128)(4,1)} %bitcast.410), calls=%async_computation.22 | async-start | bytes 4194304
  229.1 39.1 %slice-start.21 = ((s8[18874368]{0:T(1024)(128)(4,1)}), s8[4194304]{0:T(1024)(128)(4,1)S(1)}, s32[]{:S(2)}) async-start(s8[18874368]{0:T(1024)(128)(4,1)} %bitcast.410), calls=%async_computation.23 | async-start | bytes 8388608
  240.4 27.9 %slice-start.22 = ((s8[18874368]{0:T(1024)(128)(4,1)}), s8[4194304]{0:T(1024)(128)(4,1)S(1)}, s32[]{:S(2)}) async-start(s8[18874368]{0:T(1024)(128)(4,1)} %bitcast.410), calls=%async_computation.24 | async-start | bytes 8388608
  240.4 27.9 %slice-start.23 = ((s8[18874368]{0:T(1024)(128)(4,1)}), s8[4194304]{0:T(1024)(128)(4,1)S(1)}, s32[]{:S(2)}) async-start(s8[18874368]{0:T(1024)(128)(4,1)} %bitcast.410), calls=%async_computation.25 | async-start | bytes 8388608
  240.4 27.9 %slice-start.24 = ((s8[18874368]{0:T(1024)(128)(4,1)}), s8[4194304]{0:T(1024)(128)(4,1)S(1)}, s32[]{:S(2)}) async-start(s8[18874368]{0:T(1024)(128)(4,1)} %bitcast.410), calls=%async_computation.26 | async-start | bytes 8388608
  240.4 27.9 %copy-start.34 = (bf16[1536,128]{1,0:T(8,128)(2,1)S(1)}, bf16[1536,128]{1,0:T(8,128)(2,1)}, u32[]{:S(2)}) copy-start(bf16[1536,128]{1,0:T(8,128)(2,1)} %get-tuple-element.338) | copy-start | bytes 1179652
  281.6 15.5 %copy-start.32 = (bf16[1536,128]{1,0:T(8,128)(2,1)S(1)}, bf16[1536,128]{1,0:T(8,128)(2,1)}, u32[]{:S(2)}) copy-start(bf16[1536,128]{1,0:T(8,128)(2,1)} %get-tuple-element.337) | copy-start | bytes 1179652
  281.6 25.8 %slice-start.10 = ((s8[18874368]{0:T(1024)(128)(4,1)}), s8[2097152]{0:T(1024)(128)(4,1)S(1)}, s32[]{:S(2)}) async-start(s8[18874368]{0:T(1024)(128)(4,1)} %bitcast.400), calls=%async_computation.12 | async-start | bytes 4194304
  281.6 25.8 %slice-start.11 = ((s8[18874368]{0:T(1024)(128)(4,1)}), s8[4194304]{0:T(1024)(128)(4,1)S(1)}, s32[]{:S(2)}) async-start(s8[18874368]{0:T(1024)(128)(4,1)} %bitcast.400), calls=%async_computation.13 | async-start | bytes 8388608
  281.6 25.7 %slice-start.12 = ((s8[18874368]{0:T(1024)(128)(4,1)}), s8[4194304]{0:T(1024)(128)(4,1)S(1)}, s32[]{:S(2)}) async-start(s8[18874368]{0:T(1024)(128)(4,1)} %bitcast.400), calls=%async_computation.14 | async-start | bytes 8388608
  297.1 10.3 %slice-start.13 = ((s8[18874368]{0:T(1024)(128)(4,1)}), s8[4194304]{0:T(1024)(128)(4,1)S(1)}, s32[]{:S(2)}) async-start(s8[18874368]{0:T(1024)(128)(4,1)} %bitcast.400), calls=%async_computation.15 | async-start | bytes 8388608
  297.1 10.7 %slice-start.14 = ((s8[18874368]{0:T(1024)(128)(4,1)}), s8[4194304]{0:T(1024)(128)(4,1)S(1)}, s32[]{:S(2)}) async-start(s8[18874368]{0:T(1024)(128)(4,1)} %bitcast.400), calls=%async_computation.16 | async-start | bytes 8388608
  314.9 15.7 %copy-start.30 = (bf16[1536,128]{1,0:T(8,128)(2,1)S(1)}, bf16[1536,128]{1,0:T(8,128)(2,1)}, u32[]{:S(2)}) copy-start(bf16[1536,128]{1,0:T(8,128)(2,1)} %copy-done.29) | copy-start | bytes 1179652
  314.9 26.0 %slice-start.5 = ((s8[18874368]{0:T(1024)(128)(4,1)}), s8[2097152]{0:T(1024)(128)(4,1)S(1)}, s32[]{:S(2)}) async-start(s8[18874368]{0:T(1024)(128)(4,1)} %bitcast.398), calls=%async_computation.7 | async-start | bytes 4194304
  314.9 26.0 %slice-start.6 = ((s8[18874368]{0:T(1024)(128)(4,1)}), s8[4194304]{0:T(1024)(128)(4,1)S(1)}, s32[]{:S(2)}) async-start(s8[18874368]{0:T(1024)(128)(4,1)} %bitcast.398), calls=%async_computation.8 | async-start | bytes 8388608
  314.9 26.0 %slice-start.7 = ((s8[18874368]{0:T(1024)(128)(4,1)}), s8[4194304]{0:T(1024)(128)(4,1)S(1)}, s32[]{:S(2)}) async-start(s8[18874368]{0:T(1024)(128)(4,1)} %bitcast.398), calls=%async_computation.9 | async-start | bytes 8388608
  330.6 10.3 %slice-start.8 = ((s8[18874368]{0:T(1024)(128)(4,1)}), s8[4194304]{0:T(1024)(128)(4,1)S(1)}, s32[]{:S(2)}) async-start(s8[18874368]{0:T(1024)(128)(4,1)} %bitcast.398), calls=%async_computation.10 | async-start | bytes 8388608
  330.6 10.7 %slice-start.9 = ((s8[18874368]{0:T(1024)(128)(4,1)}), s8[4194304]{0:T(1024)(128)(4,1)S(1)}, s32[]{:S(2)}) async-start(s8[18874368]{0:T(1024)(128)(4,1)} %bitcast.398), calls=%async_computation.11 | async-start | bytes 8388608
  348.4 15.5 %copy-start.27 = (bf16[1536,128]{1,0:T(8,128)(2,1)S(1)}, bf16[1536,128]{1,0:T(8,128)(2,1)}, u32[]{:S(2)}) copy-start(bf16[1536,128]{1,0:T(8,128)(2,1)} %copy-done.26) | copy-start | bytes 1179652
  348.4 25.8 %slice-start = ((s8[18874368]{0:T(1024)(128)(4,1)}), s8[2097152]{0:T(1024)(128)(4,1)S(1)}, s32[]{:S(2)}) async-start(s8[18874368]{0:T(1024)(128)(4,1)} %bitcast.396), calls=%async_computation.2 | async-start | bytes 4194304
  348.4 25.8 %slice-start.1 = ((s8[18874368]{0:T(1024)(128)(4,1)}), s8[4194304]{0:T(1024)(128)(4,1)S(1)}, s32[]{:S(2)}) async-start(s8[18874368]{0:T(1024)(128)(4,1)} %bitcast.396), calls=%async_computation.3 | async-start | bytes 8388608
  348.4 25.8 %slice-start.2 = ((s8[18874368]{0:T(1024)(128)(4,1)}), s8[4194304]{0:T(1024)(128)(4,1)S(1)}, s32[]{:S(2)}) async-start(s8[18874368]{0:T(1024)(128)(4,1)} %bitcast.396), calls=%async_computation.4 | async-start | bytes 8388608
  363.9 10.3 %slice-start.3 = ((s8[18874368]{0:T(1024)(128)(4,1)}), s8[4194304]{0:T(1024)(128)(4,1)S(1)}, s32[]{:S(2)}) async-start(s8[18874368]{0:T(1024)(128)(4,1)} %bitcast.396), calls=%async_computation.5 | async-start | bytes 8388608
  363.9 10.7 %slice-start.4 = ((s8[18874368]{0:T(1024)(128)(4,1)}), s8[4194304]{0:T(1024)(128)(4,1)S(1)}, s32[]{:S(2)}) async-start(s8[18874368]{0:T(1024)(128)(4,1)} %bitcast.396), calls=%async_computation.6 | async-start | bytes 8388608
  382.0 15.5 %copy-start.24 = (bf16[1536,128]{1,0:T(8,128)(2,1)S(1)}, bf16[1536,128]{1,0:T(8,128)(2,1)}, u32[]{:S(2)}) copy-start(bf16[1536,128]{1,0:T(8,128)(2,1)} %copy-done.23) | copy-start | bytes 1179652
  382.0 15.5 %copy-start.44 = (f32[4,384]{1,0:T(4,128)S(1)}, f32[4,384]{1,0:T(4,128)}, u32[]{:S(2)}) copy-start(f32[4,384]{1,0:T(4,128)} %get-tuple-element.380) | copy-start | bytes 18436
  382.0 25.8 %slice-start.15 = ((s8[18874368]{0:T(1024)(128)(4,1)}), s8[2097152]{0:T(1024)(128)(4,1)S(1)}, s32[]{:S(2)}) async-start(s8[18874368]{0:T(1024)(128)(4,1)} %bitcast.408), calls=%async_computation.17 | async-start | bytes 4194304
  382.0 25.8 %slice-start.16 = ((s8[18874368]{0:T(1024)(128)(4,1)}), s8[4194304]{0:T(1024)(128)(4,1)S(1)}, s32[]{:S(2)}) async-start(s8[18874368]{0:T(1024)(128)(4,1)} %bitcast.408), calls=%async_computation.18 | async-start | bytes 8388608
  382.1 25.8 %slice-start.17 = ((s8[18874368]{0:T(1024)(128)(4,1)}), s8[4194304]{0:T(1024)(128)(4,1)S(1)}, s32[]{:S(2)}) async-start(s8[18874368]{0:T(1024)(128)(4,1)} %bitcast.408), calls=%async_computation.19 | async-start | bytes 8388608
  397.5 10.3 %slice-start.18 = ((s8[18874368]{0:T(1024)(128)(4,1)}), s8[4194304]{0:T(1024)(128)(4,1)S(1)}, s32[]{:S(2)}) async-start(s8[18874368]{0:T(1024)(128)(4,1)} %bitcast.408), calls=%async_computation.20 | async-start | bytes 8388608
  397.5 10.7 %slice-start.19 = ((s8[18874368]{0:T(1024)(128)(4,1)}), s8[4194304]{0:T(1024)(128)(4,1)S(1)}, s32[]{:S(2)}) async-start(s8[18874368]{0:T(1024)(128)(4,1)} %bitcast.408), calls=%async_computation.21 | async-start | bytes 8388608
  415.4 14.6 %copy-start.40 = (s32[32]{0:T(128)S(1)}, s32[32]{0:T(128)}, u32[]{:S(2)}) copy-start(s32[32]{0:T(128)} %fusion.121) | copy-start | bytes 388
  430.0 11.8 %copy-start.19 = (bf16[1536,128]{1,0:T(8,128)(2,1)S(1)}, bf16[1536,128]{1,0:T(8,128)(2,1)}, u32[]{:S(2)}) copy-start(bf16[1536,128]{1,0:T(8,128)(2,1)} %get-tuple-element.352) | copy-start | bytes 1179652
  451.0 11.7 %copy-start.39 = (bf16[1536,128]{1,0:T(8,128)(2,1)S(1)}, bf16[1536,128]{1,0:T(8,128)(2,1)}, u32[]{:S(2)}) copy-start(bf16[1536,128]{1,0:T(8,128)(2,1)} %get-tuple-element.343) | copy-start | bytes 1179652
  461.0 11.0 %slice-start.25 = ((s8[9437184]{0:T(1024)(128)(4,1)}), s8[4194304]{0:T(1024)(128)(4,1)S(1)}, s32[]{:S(2)}) async-start(s8[9437184]{0:T(1024)(128)(4,1)} %bitcast.440), calls=%async_computation.27 | async-start | bytes 8388608
  462.6 14.1 %slice-start.28 = ((s8[9437184]{0:T(1024)(128)(4,1)}), s8[4194304]{0:T(1024)(128)(4,1)S(1)}, s32[]{:S(2)}) async-start(s8[9437184]{0:T(1024)(128)(4,1)} %bitcast.442), calls=%async_computation.30 | async-start | bytes 8388608
  462.6 14.1 %slice-start.29 = ((s8[9437184]{0:T(1024)(128)(4,1)}), s8[4194304]{0:T(1024)(128)(4,1)S(1)}, s32[]{:S(2)}) async-start(s8[9437184]{0:T(1024)(128)(4,1)} %bitcast.442), calls=%async_computation.31 | async-start | bytes 8388608
  472.1 10.6 %slice-start.31 = ((s8[9437184]{0:T(1024)(128)(4,1)}), s8[4194304]{0:T(1024)(128)(4,1)S(1)}, s32[]{:S(2)}) async-start(s8[9437184]{0:T(1024)(128)(4,1)} %bitcast.444), calls=%async_computation.33 | async-start | bytes 8388608
  472.1 10.6 %slice-start.32 = ((s8[9437184]{0:T(1024)(128)(4,1)}), s8[4194304]{0:T(1024)(128)(4,1)S(1)}, s32[]{:S(2)}) async-start(s8[9437184]{0:T(1024)(128)(4,1)} %bitcast.444), calls=%async_computation.34 | async-start | bytes 8388608
  476.8 10.5 %slice-start.34 = ((s8[9437184]{0:T(1024)(128)(4,1)}), s8[4194304]{0:T(1024)(128)(4,1)S(1)}, s32[]{:S(2)}) async-start(s8[9437184]{0:T(1024)(128)(4,1)} %bitcast.446), calls=%async_computation.36 | async-start | bytes 8388608
  476.8 10.5 %slice-start.35 = ((s8[9437184]{0:T(1024)(128)(4,1)}), s8[4194304]{0:T(1024)(128)(4,1)S(1)}, s32[]{:S(2)}) async-start(s8[9437184]{0:T(1024)(128)(4,1)} %bitcast.446), calls=%async_computation.37 | async-start | bytes 8388608
  619.3 106.5 %collective-permute-start.2 = (f32[2,6,4,384,128]{4,3,2,1,0:T(8,128)}, f32[2,6,4,384,128]{4,3,2,1,0:T(8,128)}, u32[]{:S(2)}, u32[]{:S(2)}) collective-permute-start(f32[2,6,4,384,128]{4,3,2,1,0:T(8,128)} %fusion.30), channel_id=1, source_target_pairs={{0,4},{4,8},{8,12},{12,16},{16,20},{20,24},{24,28},{1,5},{5,9},{9,... | collective-permute-start | bytes 28311560 | tf_op jit(solution)/shard_map/ppermute | solution.py:30
  623.9 63.4 %all-to-all-start = ((bf16[4,384,768]{1,2,0:T(8,128)(2,1)}), bf16[4,384,768]{1,2,0:T(8,128)(2,1)S(1)}, u32[]{:S(2)}, u32[]{:S(2)}) async-start(bf16[4,384,768]{1,2,0:T(8,128)(2,1)} %get-tuple-element.378), calls=%async_computation | async-start | bytes 4718592 | tf_op jit(solution)/shard_map/all_to_all | solution.py:153
  627.6 10.4 %copy-start.8 = (bf16[32,384,128]{2,1,0:T(8,128)(2,1)S(1)}, bf16[32,384,128]{2,1,0:T(8,128)(2,1)}, u32[]{:S(2)}) copy-start(bf16[32,384,128]{2,1,0:T(8,128)(2,1)} %gather_fusion) | copy-start | bytes 9437188
  634.5 55.7 %collective-permute-start.3 = (bf16[2,6,4,384,128]{4,3,2,1,0:T(8,128)(2,1)}, bf16[2,6,4,384,128]{4,3,2,1,0:T(8,128)(2,1)}, u32[]{:S(2)}, u32[]{:S(2)}) collective-permute-start(bf16[2,6,4,384,128]{4,3,2,1,0:T(8,128)(2,1)} %fusion.35), channel_id=1, source_target_pairs={{4,0},{8,4},{12,8},{16,12},{20,16},{24,20},{28,24},{5,1},{9,5},{13... | collective-permute-start | bytes 14155784 | tf_op jit(solution)/shard_map/ppermute | solution.py:30
  645.2 9.7 %copy-start.7 = (bf16[32,384,128]{2,1,0:T(8,128)(2,1)S(1)}, bf16[32,384,128]{2,1,0:T(8,128)(2,1)}, u32[]{:S(2)}) copy-start(bf16[32,384,128]{2,1,0:T(8,128)(2,1)} %gather_fusion.4) | copy-start | bytes 9437188
  (25 other events, 178.1 us)
where the time goes:
time: 754 us; the launch traced here: 743 us
  matrix products  362 us (48%)
  other arithmetic  187 us (25%)
  local copies, waits for them, and re-layouts  109 us (14%)
  waiting for transfers between devices  59.2 us (8%)
  starting transfers between devices  22 us (3%)
    scatter-add x12, other arithmetic, add_to_tiles(): jnp.zeros((tile_count, tile_rows, head_cols), jnp.float32).at[flat_index]  121 us
    dot_general x6, matrix products, masked_scores(): jnp.einsum('aqd,astd->aqst', query_tiles, key_sel, preferred_element_type...  88.2 us
    dot_general x6, matrix products, backward_tiles(): jnp.einsum('aqd,astd->aqst', grad_tiles, value_sel, preferred_element_typ...  87.6 us
    dot_general x6, matrix products, backward_tiles(): jnp.einsum('aqst,aqd->astd', weights_low, grad_tiles, preferred_element_t...  57.6 us
    dot_general x6, matrix products, forward_tiles(): jnp.einsum('aqst,astd->aqd', weights, value_sel, preferred_element_type=j...  46.1 us
    dot_general x6, matrix products, backward_tiles(): jnp.einsum('aqst,astd->aqd', grad_scores, key_sel, preferred_element_type...  44.6 us
    dot_general x6, matrix products, backward_tiles(): jnp.einsum('aqst,aqd->astd', grad_scores, query_tiles, preferred_element_...  38.3 us
    ppermute x2, waiting for transfers between devices, from_behind(): return lax.ppermute(block, axis, route)  35.7 us
  transfers between devices with their start and end apart: 6, of which 4 were waited for; matrix products, arithmetic and copies ran while one was open for 11% of the time, Pallas kernels for 0%

commit v1 on v0

v1 whole, which is shorter than its diff:
```python
import functools
import math

import jax
import jax.numpy as jnp
from jax import lax
from jax.experimental import pallas as pl
from jax.experimental.pallas import tpu as pltpu
from jax.sharding import PartitionSpec as P

HD = 128
TILE = 384
SPT = 4
KSLOT = 8
SCALE = 1.0 / math.sqrt(HD)
EXP2_SCALE = SCALE * math.log2(math.e)


def dot_nn(a, b):
    return lax.dot_general(a, b, (((1,), (0,)), ((), ())), preferred_element_type=jnp.float32)


def dot_nt(a, b):
    return lax.dot_general(a, b, (((1,), (1,)), ((), ())), preferred_element_type=jnp.float32)


def fold_rows(block, op):
    return op(block.reshape(TILE // 8, 8, TILE), axis=0)


def attention_kernel(
    heads, own_tiles, first_col,
    idx_ref, cnt_ref, q_ref, do_ref, k_hbm, v_hbm, low_hbm, high_hbm,
    o_ref, dq_ref, dk_own, dv_own, low_out, high_out,
    kext, vext, kt, vt, scores, dk, dv, o_acc, dq_acc, sems,
):
    a = pl.program_id(0)
    ext_tiles = own_tiles + 2 * SPT
    width = heads * HD
    cols = [slice(h * HD, (h + 1) * HD) for h in range(heads)]

    @pl.when(a == 0)
    def _():
        copies = []
        for n, (dst, own_src, part) in enumerate(((kext, k_hbm, 0), (vext, v_hbm, 1))):
            rim = pl.ds(part * width, width)
            copies.append(pltpu.make_async_copy(
                low_hbm.at[:, :, rim], dst.at[pl.ds(0, SPT)], sems.at[3 * n]))
            copies.append(pltpu.make_async_copy(
                own_src.at[:, :, pl.ds(first_col, width)], dst.at[pl.ds(SPT, own_tiles)],
                sems.at[3 * n + 1]))
            copies.append(pltpu.make_async_copy(
                high_hbm.at[:, :, rim], dst.at[pl.ds(SPT + own_tiles, SPT)], sems.at[3 * n + 2]))
        for copy in copies:
            copy.start()
        dk[...] = jnp.zeros_like(dk)
        dv[...] = jnp.zeros_like(dv)
        for copy in copies:
            copy.wait()

        @pl.loop(0, ext_tiles)
        def _(t):
            for h in range(heads):
                kt[h, t] = kext[t, :, cols[h]].T
                vt[h, t] = vext[t, :, cols[h]].T

    count = cnt_ref[a]

    def score_slot(s, tops):
        t = idx_ref[a * KSLOT + s]
        new = []
        for h in range(heads):
            block = dot_nt(kext[t, :, cols[h]], q_ref[:, cols[h]])
            scores[h, s] = block
            new.append(jnp.maximum(tops[h], fold_rows(block, jnp.max)))
        return tuple(new)

    tops = lax.fori_loop(
        0, count, score_slot, tuple(jnp.full((8, TILE), -jnp.inf, jnp.float32) for _ in cols)
    )
    tops = [jnp.max(top, axis=0, keepdims=True) for top in tops]

    def exp_slot(s, sums):
        new = []
        for h in range(heads):
            block = jnp.exp2((scores[h, s] - tops[h]) * EXP2_SCALE)
            scores[h, s] = block
            new.append(sums[h] + fold_rows(block, jnp.sum))
        return tuple(new)

    sums = lax.fori_loop(
        0, count, exp_slot, tuple(jnp.zeros((8, TILE), jnp.float32) for _ in cols)
    )
    inverse = [1.0 / jnp.sum(total, axis=0, keepdims=True) for total in sums]

    o_acc[...] = jnp.zeros_like(o_acc)
    dq_acc[...] = jnp.zeros_like(dq_acc)

    @pl.loop(0, count)
    def _(s):
        t = idx_ref[a * KSLOT + s]
        for h in range(heads):
            weights = scores[h, s] * inverse[h]
            scores[h, s] = weights
            low = weights.astype(jnp.bfloat16)
            o_acc[h] += dot_nn(vt[h, t], low)
            dv[t, :, cols[h]] += dot_nn(low, do_ref[:, cols[h]])

    deltas = []
    for h in range(heads):
        out_t = o_acc[h].astype(jnp.bfloat16).astype(jnp.float32)
        grads_t = do_ref[:, cols[h]].astype(jnp.float32).T
        deltas.append(jnp.sum(out_t * grads_t, axis=0, keepdims=True))
        o_ref[:, cols[h]] = out_t.T.astype(jnp.bfloat16)

    @pl.loop(0, count)
    def _(s):
        t = idx_ref[a * KSLOT + s]
        for h in range(heads):
            grads = dot_nt(vext[t, :, cols[h]], do_ref[:, cols[h]])
            low = (scores[h, s] * (grads - deltas[h])).astype(jnp.bfloat16)
            dk[t, :, cols[h]] += dot_nn(low, q_ref[:, cols[h]])
            dq_acc[h] += dot_nn(kt[h, t], low)

    for h in range(heads):
        dq_ref[:, cols[h]] = (dq_acc[h] * SCALE).T.astype(jnp.bfloat16)

    @pl.when(a == own_tiles - 1)
    def _():
        own = pl.ds(SPT, own_tiles)

        @pl.loop(0, ext_tiles)
        def _(t):
            scaled = dk[t] * SCALE
            dk[t] = scaled
            kext[t] = scaled.astype(jnp.bfloat16)
            vext[t] = dv[t].astype(jnp.bfloat16)

        copies = []
        for n, (src, wide, own_dst, part) in enumerate(
            ((kext, dk, dk_own, 0), (vext, dv, dv_own, 1))
        ):
            rim = pl.ds(part * width, width)
            copies.append(pltpu.make_async_copy(
                src.at[pl.ds(0, SPT)], low_out.at[:, :, rim], sems.at[3 * n]))
            copies.append(pltpu.make_async_copy(wide.at[own], own_dst, sems.at[3 * n + 1]))
            copies.append(pltpu.make_async_copy(
                src.at[pl.ds(SPT + own_tiles, SPT)], high_out.at[:, :, rim], sems.at[3 * n + 2]))
        for copy in copies:
            copy.start()
        for copy in copies:
            copy.wait()


def attention(heads, first_col, idx, cnt, queries, grads, keys, values, low, high):
    rows, _ = queries.shape
    own_tiles = rows // TILE
    ext_tiles = own_tiles + 2 * SPT
    width = heads * HD
    col_block = first_col // width
    assert col_block * width == first_col
    smem = pl.BlockSpec(memory_space=pltpu.SMEM)
    hbm = pl.BlockSpec(memory_space=pl.ANY)
    rim = jax.ShapeDtypeStruct((SPT, TILE, 2 * width), jnp.bfloat16)
    own = jax.ShapeDtypeStruct((own_tiles, TILE, width), jnp.float32)
    token_rows = jax.ShapeDtypeStruct((rows, width), jnp.bfloat16)
    row_block = pl.BlockSpec((TILE, width), lambda a: (a, 0))
    pairs = own_tiles * 6 * heads
    return pl.pallas_call(
        functools.partial(attention_kernel, heads, own_tiles, first_col),
        grid=(own_tiles,),
        in_specs=[
            smem, smem,
            pl.BlockSpec((TILE, width), lambda a: (a, col_block)),
            row_block, hbm, hbm, hbm, hbm,
        ],
        out_specs=[row_block, row_block, hbm, hbm, hbm, hbm],
        out_shape=[token_rows, token_rows, own, own, rim, rim],
        scratch_shapes=[
            pltpu.VMEM((ext_tiles, TILE, width), jnp.bfloat16),
            pltpu.VMEM((ext_tiles, TILE, width), jnp.bfloat16),
            pltpu.VMEM((heads, ext_tiles, HD, TILE), jnp.bfloat16),
            pltpu.VMEM((heads, ext_tiles, HD, TILE), jnp.bfloat16),
            pltpu.VMEM((heads, KSLOT, TILE, TILE), jnp.float32),
            pltpu.VMEM((ext_tiles, TILE, width), jnp.float32),
            pltpu.VMEM((ext_tiles, TILE, width), jnp.float32),
            pltpu.VMEM((heads, HD, TILE), jnp.float32),
            pltpu.VMEM((heads, HD, TILE), jnp.float32),
            pltpu.SemaphoreType.DMA((6,)),
        ],
        compiler_params=pltpu.CompilerParams(vmem_limit_bytes=56 * 1024 * 1024),
        cost_estimate=pl.CostEstimate(
            flops=pairs * 30 * TILE * TILE * HD,
            bytes_accessed=30 * rows * width,
            transcendentals=pairs * TILE * TILE,
        ),
    )(idx, cnt, queries, grads, keys, values, low, high)


def neighbours(axis):
    count = lax.axis_size(axis)
    up = [(i, i + 1) for i in range(count - 1)]
    return up, [(b, a) for a, b in up]


def scatter_heads(block):
    return lax.all_to_all(block, "head", split_axis=1, concat_axis=0, tiled=True)


def gather_heads(block):
    return lax.all_to_all(block, "head", split_axis=0, concat_axis=1, tiled=True)


def head_groups(heads_here):
    size = 2
    groups, start = [], 0
    while start < heads_here:
        groups.append((start, min(size, heads_here - start)))
        start += size
    return groups


def shards(queries, key_states, value_states, out_grads, pattern):
    row_count, col_count = queries.shape
    heads_here = col_count // HD
    rim_rows = SPT * TILE
    own_tiles = row_count // TILE
    head_devices = lax.axis_size("head")
    own_rows = out_grads.shape[0]
    first_tile = lax.axis_index("ctx") * own_tiles
    listed = lax.dynamic_slice_in_dim(pattern, first_tile, own_tiles, 0)
    allowed = listed >= 0
    idx = jnp.where(allowed, listed - (first_tile - SPT), 0).reshape(-1).astype(jnp.int32)
    cnt = jnp.sum(allowed.astype(jnp.int32), axis=1)
    up, down = neighbours("ctx")
    groups = head_groups(heads_here)
    keys_tiled = key_states.reshape(own_tiles, TILE, col_count)
    values_tiled = value_states.reshape(own_tiles, TILE, col_count)
    by_head = out_grads.reshape(own_rows, head_devices, col_count)

    lows, highs, grads = [], [], []
    for start, heads in groups:
        cols = slice(start * HD, (start + heads) * HD)
        packed = jnp.concatenate((keys_tiled[:, :, cols], values_tiled[:, :, cols]), axis=2)
        if lows:
            packed, lows[-1], highs[-1] = lax.optimization_barrier((packed, lows[-1], highs[-1]))
        lows.append(lax.ppermute(packed[own_tiles - SPT:], "ctx", up))
        highs.append(lax.ppermute(packed[:SPT], "ctx", down))
        grads.append(scatter_heads(by_head[:, :, cols].reshape(own_rows, -1)))

    attended, query_grads, key_grads, value_grads = [], [], [], []
    for group, (start, heads) in enumerate(groups):
        width = heads * HD
        out, dq, dk, dv, low, high = attention(
            heads, start * HD, idx, cnt, queries, grads[group], keys_tiled, values_tiled,
            lows[group], highs[group],
        )
        attended.append(gather_heads(out).reshape(own_rows, head_devices, width))
        query_grads.append(dq)
        from_above = lax.ppermute(low, "ctx", down)
        from_below = lax.ppermute(high, "ctx", up)
        for own, part, sums in ((dk, 0, key_grads), (dv, 1, value_grads)):
            cols = slice(part * width, (part + 1) * width)
            above = from_above[:, :, cols].astype(jnp.float32)
            below = from_below[:, :, cols].astype(jnp.float32)
            if own_tiles > SPT:
                extra = ((0, own_tiles - SPT), (0, 0), (0, 0))
                below = jnp.pad(below, extra)
                above = jnp.pad(above, (extra[0][::-1], (0, 0), (0, 0)))
            total = own + above + below
            sums.append(total.astype(jnp.bfloat16).reshape(row_count, width))
    return (
        jnp.concatenate(attended, axis=2).reshape(own_rows, head_devices * col_count),
        jnp.concatenate(query_grads, axis=1),
        jnp.concatenate(key_grads, axis=1),
        jnp.concatenate(value_grads, axis=1),
    )


def solution(mesh):
    return jax.shard_map(
        shards,
        mesh=mesh,
        in_specs=(
            P("ctx", "head"),
            P("ctx", "head"),
            P("ctx", "head"),
            P(("ctx", "head"), None),
            P(),
        ),
        out_specs=(P(("ctx", "head"), None), P("ctx", "head"), P("ctx", "head"), P("ctx", "head")),
        check_vma=False,
    )
```

time: 754 us -> 276 us (0.37)
  matrix products: 362 us -> 0 us
  other arithmetic: 187 us -> 20.4 us
  Pallas kernels: 0 us -> 137 us
  local copies, waits for them, and re-layouts: 109 us -> 17.6 us
  starting transfers between devices: 22 us -> 81.7 us
  waiting for transfers between devices: 59.2 us -> 13.3 us
    dot_general x36 -> x0, matrix products: 362 us -> none  [the longest x6 88.2 us: masked_scores(): jnp.einsum('aqd,astd->aqst', query_tiles, key_sel, preferred_element_type...]
    pallas_call x0 -> x3, Pallas kernels: none -> 137 us  [attention(): pl.pallas_call(functools.partial(attention_kernel, heads, own_tiles, firs...]
    scatter-add x12 -> x0, other arithmetic: 121 us -> none  [add_to_tiles(): jnp.zeros((tile_count, tile_rows, head_cols), jnp.float32).at[flat_index]]
    ppermute x4 -> x12, starting transfers between devices: 14.7 us -> 59.8 us  [the longest x3 35.8 us: shards(): from_above = lax.ppermute(low, 'ctx', down)]
    gather x12 -> x0, local copies, waits for them, and re-layouts: 42.9 us -> none  [the longest x6 23.3 us: forward_tiles(): key_sel = jnp.take(key_tiles, slot_index, axis=0)]
    ppermute x4 -> x12, waiting for transfers between devices: 36.4 us -> 4.02 us  [the longest x3 3.99 us: shards(): highs.append(lax.ppermute(packed[:SPT], 'ctx', down))]
    unnamed x187 -> x35, local copies, waits for them, and re-layouts: 35.5 us -> 4.73 us
    reduce_sum x7 -> x1, other arithmetic: 28.5 us -> 0.62 us  [shards(): cnt = jnp.sum(allowed.astype(jnp.int32), axis=1)]
  transfers between devices with their start and end apart: 6 -> 18, of which waited for: 4 -> 3; matrix products, arithmetic and copies ran while one was open for 11% -> 9% of each run, Pallas kernels for 0% -> 51%
where the time goes in v1:
time: 276 us; the launch traced here: 271 us
  Pallas kernels  137 us (50%)
  starting transfers between devices  81.7 us (30%)
  other arithmetic  20.4 us (7%)
  local copies, waits for them, and re-layouts  17.6 us (6%)
  waiting for transfers between devices  13.3 us (5%)
    pallas_call x3, Pallas kernels, attention(): pl.pallas_call(functools.partial(attention_kernel, heads, own_tiles, firs...  137 us
    ppermute x3, starting transfers between devices, shards(): from_above = lax.ppermute(low, 'ctx', down)  35.8 us
    all_to_all x3, starting transfers between devices, gather_heads(): lax.all_to_all(block, 'head', split_axis=0, concat_axis=1, tiled=True)  11 us
    all_to_all x3, starting transfers between devices, scatter_heads(): lax.all_to_all(block, 'head', split_axis=1, concat_axis=0, tiled=True)  10.9 us
    convert_element_type x3, other arithmetic, shards(): sums.append(total.astype(jnp.bfloat16).reshape(row_count, width))  10.4 us
    ppermute x3, starting transfers between devices, shards(): highs.append(lax.ppermute(packed[:SPT], 'ctx', down))  9.57 us
    all_to_all x3, waiting for transfers between devices, gather_heads(): lax.all_to_all(block, 'head', split_axis=0, concat_axis=1, tiled=True)  9.26 us
    ppermute x3, starting transfers between devices, shards(): lows.append(lax.ppermute(packed[own_tiles - SPT:], 'ctx', up))  8.42 us
  transfers between devices with their start and end apart: 18, of which 3 were waited for; matrix products, arithmetic and copies ran while one was open for 9% of the time, Pallas kernels for 51%

profile of v1, /device:TPU:1, one launch (start us, length us, event | category | flops | bytes accessed | tf_op | source)
XLA Modules:
  0.0 271.0 jit_solution(5840487011169567813)
XLA Ops:
  0.6 4.2 %fusion.1 = (bf16[4,384,256]{2,1,0:T(8,128)(2,1)S(1)}, bf16[4,384,256]{2,1,0:T(8,128)(2,1)}, bf16[4,384,256]{2,1,0:T(8,128)(2,1)}, bf16[4,384,256]{2,1,0:T(8,128...) fusion(bf16[4,384,768]{2,1,0:T(8,128)(2,1)} %bitcast.36, bf16[4,384,768]{2,1,0:T(8,128)(2,1)} %bitcast.40), kind=kLoop, calls=%fused_computation.17 | loop fusion | bytes 9437184 | tf_op jit(solution)/shard_map/slice | solution.py:244
  4.8 1.3 pad_maximum_fusion.4
  6.1 4.6 %collective-permute-start = (bf16[4,384,512]{2,1,0:T(8,128)(2,1)}, bf16[4,384,512]{2,1,0:T(8,128)(2,1)}, u32[]{:S(2)}, u32[]{:S(2)}) collective-permute-start(bf16[4,384,512]{2,1,0:T(8,128)(2,1)} %pad_maximum_fusion.4), channel_id=1, source_target_pairs={{0,4},{4,8},{8,12},{12,16},{16,20},{20,24},{24,28},{1,5},{5,9},{9,... | collective-permute-start | bytes 4718600 | tf_op jit(solution)/shard_map/ppermute | solution.py:247
  10.7 1.9 collective-permute-start.1
  12.6 4.5 %reshape.72 = bf16[384,4,768]{2,1,0:T(4,128)(2,1)S(1)} reshape(bf16[384,3072]{1,0:T(8,128)(2,1)} %param.8) | data formatting | bytes 4718592 | tf_op jit(solution)/shard_map/reshape | solution.py:239
  17.1 1.7 fusion
  18.8 1.0 copy.14
  19.8 3.5 %all-to-all-start = ((bf16[384,4,256]{2,0,1:T(8,128)(2,1)}), bf16[384,4,256]{2,0,1:T(8,128)(2,1)S(1)}, u32[]{:S(2)}, u32[]{:S(2)}) async-start(bf16[384,4,256]{2,0,1:T(8,128)(2,1)} %copy.14), calls=%async_computation | async-start | bytes 1572864 | tf_op jit(solution)/shard_map/all_to_all | solution.py:207
  23.4 0.6 convert_reduce_fusion
  24.0 0.1 subtract_select_fusion
  24.1 0.1 copy.9
  24.1 0.7 reshape.71.idx_ref
  24.8 1.0 copy.15
  25.8 1.0 copy.16
  26.9 1.3 pad_maximum_fusion.3
  28.1 0.0 copy-done.1
  28.2 0.6 copy-done.2
  28.8 0.1 pad_maximum_fusion.5
  28.9 0.0 collective-permute-done.low_hbm
  28.9 4.0 %collective-permute-done.1.high_hbm = bf16[4,384,512]{2,1,0:T(8,128)(2,1)} collective-permute-done((bf16[4,384,512]{2,1,0:T(8,128)(2,1)}, bf16[4,384,512]{2,1,0:T(8,128)(2,1)}, u32[]{:S(2)}, u32[]{:S(2)}) %collective-permute-start.1) | collective-permute-done | bytes 1572896 | tf_op jit(solution)/shard_map/ppermute | solution.py:248
  32.9 1.9 collective-permute-start.2
  34.8 3.6 %collective-permute-start.3 = (bf16[4,384,512]{2,1,0:T(8,128)(2,1)}, bf16[4,384,512]{2,1,0:T(8,128)(2,1)}, u32[]{:S(2)}, u32[]{:S(2)}) collective-permute-start(bf16[4,384,512]{2,1,0:T(8,128)(2,1)} %pad_maximum_fusion.3), channel_id=1, source_target_pairs={{4,0},{8,4},{12,8},{16,12},{20,16},{24,20},{28,24},{5,1},{9,5},{13... | collective-permute-start | bytes 4718600 | tf_op jit(solution)/shard_map/ppermute | solution.py:248
  38.4 0.0 all-to-all-done
  38.4 0.0 copy-start.12
  38.4 3.5 %all-to-all-start.2 = ((bf16[384,4,256]{2,0,1:T(8,128)(2,1)}), bf16[384,4,256]{2,0,1:T(8,128)(2,1)S(1)}, u32[]{:S(2)}, u32[]{:S(2)}) async-start(bf16[384,4,256]{2,0,1:T(8,128)(2,1)} %copy.15), calls=%async_computation.2 | async-start | bytes 1572864 | tf_op jit(solution)/shard_map/all_to_all | solution.py:207
  41.9 45.7 %shard_map.84 = (bf16[1536,256]{1,0:T(8,128)(2,1)}, bf16[1536,256]{1,0:T(8,128)(2,1)}, f32[4,384,256]{2,1,0:T(8,128)}, f32[4,384,256]{2,1,0:T(8,128)}, bf16[4,38...) custom-call(s32[32]{0:T(128)} %reshape.71.idx_ref, s32[4]{0:T(128)} %get-tuple-element.52.cnt_ref, ...), custom_call_target="tpu_custom_call" | custom-call | flops 27179089920 | bytes 11796480 | tf_op jit(solution)/shard_map/pallas_call | solution.py:169
  87.6 11.3 %collective-permute-start.6 = (bf16[4,384,512]{2,1,0:T(8,128)(2,1)}, bf16[4,384,512]{2,1,0:T(8,128)(2,1)}, u32[]{:S(2)}, u32[]{:S(2)}) collective-permute-start(bf16[4,384,512]{2,1,0:T(8,128)(2,1)} %get-tuple-element.41), channel_id=1, source_target_pairs={{4,0},{8,4},{12,8},{16,12},{20,16},{24,20},{28,24},{5,1},{9,5},{13... | collective-permute-start | bytes 4718600 | tf_op jit(solution)/shard_map/ppermute | solution.py:260
  98.9 1.9 collective-permute-start.7
  100.8 0.0 collective-permute-done.2.low_hbm
  100.9 0.0 collective-permute-done.3.high_hbm
  100.9 1.9 collective-permute-start.4
  102.8 4.1 %collective-permute-start.5 = (bf16[4,384,512]{2,1,0:T(8,128)(2,1)S(1)}, bf16[4,384,512]{2,1,0:T(8,128)(2,1)}, u32[]{:S(2)}, u32[]{:S(2)}) collective-permute-start(bf16[4,384,512]{2,1,0:T(8,128)(2,1)S(1)} %pad_maximum_fusion.5), channel_id=1, source_target_pairs={{4,0},{8,4},{12,8},{16,12},{20,16},{24,20},{28,24},{5,1},{9,5},{13... | collective-permute-start | bytes 4718600 | tf_op jit(solution)/shard_map/ppermute | solution.py:248
  106.9 0.0 copy-start.13
  106.9 3.9 %all-to-all-start.4 = ((bf16[384,4,256]{2,0,1:T(8,128)(2,1)}), bf16[384,4,256]{2,0,1:T(8,128)(2,1)S(1)}, u32[]{:S(2)}, u32[]{:S(2)}) async-start(bf16[384,4,256]{2,0,1:T(8,128)(2,1)} %copy.16), calls=%async_computation.4 | async-start | bytes 1572864 | tf_op jit(solution)/shard_map/all_to_all | solution.py:207
  110.8 45.7 %shard_map.85 = (bf16[1536,256]{1,0:T(8,128)(2,1)}, bf16[1536,256]{1,0:T(8,128)(2,1)}, f32[4,384,256]{2,1,0:T(8,128)}, f32[4,384,256]{2,1,0:T(8,128)}, bf16[4,38...) custom-call(s32[32]{0:T(128)} %reshape.71.idx_ref, s32[4]{0:T(128)} %get-tuple-element.52.cnt_ref, ...), custom_call_target="tpu_custom_call" | custom-call | flops 27179089920 | bytes 11796480 | tf_op jit(solution)/shard_map/pallas_call | solution.py:169
  156.6 11.4 %collective-permute-start.8 = (bf16[4,384,512]{2,1,0:T(8,128)(2,1)}, bf16[4,384,512]{2,1,0:T(8,128)(2,1)}, u32[]{:S(2)}, u32[]{:S(2)}) collective-permute-start(bf16[4,384,512]{2,1,0:T(8,128)(2,1)} %get-tuple-element.44), channel_id=1, source_target_pairs={{4,0},{8,4},{12,8},{16,12},{20,16},{24,20},{28,24},{5,1},{9,5},{13... | collective-permute-start | bytes 4718600 | tf_op jit(solution)/shard_map/ppermute | solution.py:260
  168.0 3.9 %all-to-all-start.1 = ((bf16[4,384,256]{2,1,0:T(8,128)(2,1)}), bf16[4,384,256]{2,1,0:T(8,128)(2,1)S(1)}, u32[]{:S(2)}, u32[]{:S(2)}) async-start(bf16[4,384,256]{2,1,0:T(8,128)(2,1)} %bitcast.4), calls=%async_computation.1 | async-start | bytes 1572864 | tf_op jit(solution)/shard_map/all_to_all | solution.py:211
  171.9 0.0 collective-permute-done.4.low_hbm
  171.9 2.1 collective-permute-start.9
  174.0 45.7 %shard_map.86 = (bf16[1536,256]{1,0:T(8,128)(2,1)}, bf16[1536,256]{1,0:T(8,128)(2,1)}, f32[4,384,256]{2,1,0:T(8,128)}, f32[4,384,256]{2,1,0:T(8,128)}, bf16[4,38...) custom-call(s32[32]{0:T(128)} %reshape.71.idx_ref, s32[4]{0:T(128)} %get-tuple-element.52.cnt_ref, ...), custom_call_target="tpu_custom_call" | custom-call | flops 27179089920 | bytes 11796480 | tf_op jit(solution)/shard_map/pallas_call | solution.py:169
  219.7 13.2 %collective-permute-start.10 = (bf16[4,384,512]{2,1,0:T(8,128)(2,1)}, bf16[4,384,512]{2,1,0:T(8,128)(2,1)}, u32[]{:S(2)}, u32[]{:S(2)}) collective-permute-start(bf16[4,384,512]{2,1,0:T(8,128)(2,1)} %get-tuple-element.47), channel_id=1, source_target_pairs={{4,0},{8,4},{12,8},{16,12},{20,16},{24,20},{28,24},{5,1},{9,5},{13... | collective-permute-start | bytes 4718600 | tf_op jit(solution)/shard_map/ppermute | solution.py:260
  232.9 0.0 collective-permute-done.6
  232.9 1.9 collective-permute-start.11
  234.8 0.0 all-to-all-done.1
  234.8 3.6 %all-to-all-start.3 = ((bf16[4,384,256]{2,1,0:T(8,128)(2,1)}), bf16[4,384,256]{2,1,0:T(8,128)(2,1)S(1)}, u32[]{:S(2)}, u32[]{:S(2)}) async-start(bf16[4,384,256]{2,1,0:T(8,128)(2,1)} %bitcast.8), calls=%async_computation.3 | async-start | bytes 1572864 | tf_op jit(solution)/shard_map/all_to_all | solution.py:211
  238.4 4.3 %add_convert_fusion.2 = (bf16[4,384,256]{2,1,0:T(8,128)(2,1)}, bf16[4,384,256]{2,1,0:T(8,128)(2,1)S(1)}) fusion(f32[4,384,256]{2,1,0:T(8,128)} %get-tuple-element.49, bf16[4,384,512]{2,1,0:T(8,128)(2,1)} %collective-permute-done.7, bf16[4,384,512]{2,1,0:T(8,128)(2,1)} %collective-permute-done.6, f32[4,384,256]{2,1,0:T(8,128)} %get-tuple-element.40), kind=kLoop, calls=%fused_computation.9 | loop fusion | flops 3932160 | bytes 7864320 | tf_op jit(solution)/shard_map/convert_element_type | solution.py:271
  242.7 6.0 %all-to-all-done.3 = bf16[4,384,256]{2,1,0:T(8,128)(2,1)S(1)} async-done(((bf16[4,384,256]{2,1,0:T(8,128)(2,1)}), bf16[4,384,256]{2,1,0:T(8,128)(2,1)S(1)}, u32[]{:S(2)}, u32[]{:S(2)}) %all-to-all-start.3) | async-done | bytes 786464 | tf_op jit(solution)/shard_map/all_to_all | solution.py:211
  248.7 3.5 %all-to-all-start.5 = ((bf16[4,384,256]{2,1,0:T(8,128)(2,1)}), bf16[4,384,256]{2,1,0:T(8,128)(2,1)S(1)}, u32[]{:S(2)}, u32[]{:S(2)}) async-start(bf16[4,384,256]{2,1,0:T(8,128)(2,1)} %bitcast.45), calls=%async_computation.5 | async-start | bytes 1572864 | tf_op jit(solution)/shard_map/all_to_all | solution.py:211
  252.2 0.0 copy-start.8
  252.2 3.3 %pad_maximum_fusion = bf16[1536,768]{1,0:T(8,128)(2,1)} fusion(bf16[1536,256]{1,0:T(8,128)(2,1)} %get-tuple-element.39, bf16[1536,256]{1,0:T(8,128)(2,1)} %get-tuple-element.38, bf16[1536,256]{1,0:T(8,128)(2,1)} %get-tuple-element.37), kind=kLoop, calls=%fused_computation.1 | loop fusion | flops 7077888 | bytes 4718592 | tf_op jit(solution)/shard_map/concatenate | solution.py:274
  255.6 0.0 collective-permute-done.8
  255.6 0.0 collective-permute-done.9
  255.6 3.6 %add_convert_fusion.1 = (bf16[4,384,256]{2,1,0:T(8,128)(2,1)}, bf16[4,384,256]{2,1,0:T(8,128)(2,1)}) fusion(f32[4,384,256]{2,1,0:T(8,128)S(1)} %copy-done.9, bf16[4,384,512]{2,1,0:T(8,128)(2,1)} %collective-permute-done.9, bf16[4,384,512]{2,1,0:T(8,128)(2,1)} %collective-permute-done.8, f32[4,384,256]{2,1,0:T(8,128)S(1)} %copy-done.8), kind=kLoop, calls=%fused_computation.8 | loop fusion | flops 3932160 | bytes 7864320 | tf_op jit(solution)/shard_map/convert_element_type | solution.py:271
  259.2 3.3 %all-to-all-done.5 = bf16[4,384,256]{2,1,0:T(8,128)(2,1)S(1)} async-done(((bf16[4,384,256]{2,1,0:T(8,128)(2,1)}), bf16[4,384,256]{2,1,0:T(8,128)(2,1)S(1)}, u32[]{:S(2)}, u32[]{:S(2)}) %all-to-all-start.5) | async-done | bytes 786464 | tf_op jit(solution)/shard_map/all_to_all | solution.py:211
  262.5 0.2 maximum_bitcast_fusion
  262.6 0.0 copy-start.10
  262.6 0.0 copy-start.11
  262.6 1.7 copy.17
  264.4 0.0 collective-permute-done.10
  264.4 0.0 collective-permute-done.11
  264.4 1.0 copy-done.11
  265.4 2.5 add_convert_fusion
  267.9 1.6 pad_maximum_fusion.2
  269.5 1.6 pad_maximum_fusion.1
  (28 shorter events, 0.1 us)
Async XLA Ops:
  6.1 22.8 %collective-permute-start = (bf16[4,384,512]{2,1,0:T(8,128)(2,1)}, bf16[4,384,512]{2,1,0:T(8,128)(2,1)}, u32[]{:S(2)}, u32[]{:S(2)}) collective-permute-start(bf16[4,384,512]{2,1,0:T(8,128)(2,1)} %pad_maximum_fusion.4), channel_id=1, source_target_pairs={{0,4},{4,8},{8,12},{12,16},{16,20},{20,24},{24,28},{1,5},{5,9},{9,... | collective-permute-start | bytes 4718600 | tf_op jit(solution)/shard_map/ppermute | solution.py:247
  10.7 22.2 %collective-permute-start.1 = (bf16[4,384,512]{2,1,0:T(8,128)(2,1)}, bf16[4,384,512]{2,1,0:T(8,128)(2,1)}, u32[]{:S(2)}, u32[]{:S(2)}) collective-permute-start(bf16[4,384,512]{2,1,0:T(8,128)(2,1)} %pad_maximum_fusion.4), channel_id=1, source_target_pairs={{4,0},{8,4},{12,8},{16,12},{20,16},{24,20},{28,24},{5,1},{9,5},{13... | collective-permute-start | bytes 4718600 | tf_op jit(solution)/shard_map/ppermute | solution.py:248
  18.8 4.5 %copy-start.15 = (s32[32,8]{0,1:T(8,128)S(1)}, s32[32,8]{0,1:T(8,128)}, u32[]{:S(2)}) copy-start(s32[32,8]{0,1:T(8,128)} %param.9) | copy-start | bytes 3076
  18.8 6.0 %copy-start = (bf16[384,4,256]{2,1,0:T(4,128)(2,1)S(1)}, bf16[384,4,256]{2,1,0:T(4,128)(2,1)}, u32[]{:S(2)}) copy-start(bf16[384,4,256]{2,1,0:T(4,128)(2,1)} %get-tuple-element.61) | copy-start | bytes 2359300
  19.8 18.6 %all-to-all-start = ((bf16[384,4,256]{2,0,1:T(8,128)(2,1)}), bf16[384,4,256]{2,0,1:T(8,128)(2,1)S(1)}, u32[]{:S(2)}, u32[]{:S(2)}) async-start(bf16[384,4,256]{2,0,1:T(8,128)(2,1)} %copy.14), calls=%async_computation | async-start | bytes 1572864 | tf_op jit(solution)/shard_map/all_to_all | solution.py:207
  24.8 2.0 copy-start.3
  24.8 2.0 copy-start.4
  26.8 1.3 copy-start.1
  26.8 1.9 copy-start.2
  32.9 67.9 %collective-permute-start.2 = (bf16[4,384,512]{2,1,0:T(8,128)(2,1)}, bf16[4,384,512]{2,1,0:T(8,128)(2,1)}, u32[]{:S(2)}, u32[]{:S(2)}) collective-permute-start(bf16[4,384,512]{2,1,0:T(8,128)(2,1)} %pad_maximum_fusion.3), channel_id=1, source_target_pairs={{0,4},{4,8},{8,12},{12,16},{16,20},{20,24},{24,28},{1,5},{5,9},{9,... | collective-permute-start | bytes 4718600 | tf_op jit(solution)/shard_map/ppermute | solution.py:247
  34.8 66.0 %collective-permute-start.3 = (bf16[4,384,512]{2,1,0:T(8,128)(2,1)}, bf16[4,384,512]{2,1,0:T(8,128)(2,1)}, u32[]{:S(2)}, u32[]{:S(2)}) collective-permute-start(bf16[4,384,512]{2,1,0:T(8,128)(2,1)} %pad_maximum_fusion.3), channel_id=1, source_target_pairs={{4,0},{8,4},{12,8},{16,12},{20,16},{24,20},{28,24},{5,1},{9,5},{13... | collective-permute-start | bytes 4718600 | tf_op jit(solution)/shard_map/ppermute | solution.py:248
  38.4 3.5 %copy-start.12 = (bf16[384,4,256]{2,0,1:T(8,128)(2,1)}, bf16[384,4,256]{2,0,1:T(8,128)(2,1)S(1)}, u32[]{:S(2)}) copy-start(bf16[384,4,256]{2,0,1:T(8,128)(2,1)S(1)} %all-to-all-done) | copy-start | bytes 2359300
  38.4 68.5 %all-to-all-start.2 = ((bf16[384,4,256]{2,0,1:T(8,128)(2,1)}), bf16[384,4,256]{2,0,1:T(8,128)(2,1)S(1)}, u32[]{:S(2)}, u32[]{:S(2)}) async-start(bf16[384,4,256]{2,0,1:T(8,128)(2,1)} %copy.15), calls=%async_computation.2 | async-start | bytes 1572864 | tf_op jit(solution)/shard_map/all_to_all | solution.py:207
  87.6 145.2 %collective-permute-start.6 = (bf16[4,384,512]{2,1,0:T(8,128)(2,1)}, bf16[4,384,512]{2,1,0:T(8,128)(2,1)}, u32[]{:S(2)}, u32[]{:S(2)}) collective-permute-start(bf16[4,384,512]{2,1,0:T(8,128)(2,1)} %get-tuple-element.41), channel_id=1, source_target_pairs={{4,0},{8,4},{12,8},{16,12},{20,16},{24,20},{28,24},{5,1},{9,5},{13... | collective-permute-start | bytes 4718600 | tf_op jit(solution)/shard_map/ppermute | solution.py:260
  98.9 139.5 %collective-permute-start.7 = (bf16[4,384,512]{2,1,0:T(8,128)(2,1)}, bf16[4,384,512]{2,1,0:T(8,128)(2,1)}, u32[]{:S(2)}, u32[]{:S(2)}) collective-permute-start(bf16[4,384,512]{2,1,0:T(8,128)(2,1)} %get-tuple-element.42), channel_id=1, source_target_pairs={{0,4},{4,8},{8,12},{12,16},{16,20},{20,24},{24,28},{1,5},{5,9},{9,... | collective-permute-start | bytes 4718600 | tf_op jit(solution)/shard_map/ppermute | solution.py:261
  100.9 71.0 %collective-permute-start.4 = (bf16[4,384,512]{2,1,0:T(8,128)(2,1)S(1)}, bf16[4,384,512]{2,1,0:T(8,128)(2,1)}, u32[]{:S(2)}, u32[]{:S(2)}) collective-permute-start(bf16[4,384,512]{2,1,0:T(8,128)(2,1)S(1)} %pad_maximum_fusion.5), channel_id=1, source_target_pairs={{0,4},{4,8},{8,12},{12,16},{16,20},{20,24},{24,28},{1,5},{5,9},{9,... | collective-permute-start | bytes 4718600 | tf_op jit(solution)/shard_map/ppermute | solution.py:247
  102.8 71.2 %collective-permute-start.5 = (bf16[4,384,512]{2,1,0:T(8,128)(2,1)S(1)}, bf16[4,384,512]{2,1,0:T(8,128)(2,1)}, u32[]{:S(2)}, u32[]{:S(2)}) collective-permute-start(bf16[4,384,512]{2,1,0:T(8,128)(2,1)S(1)} %pad_maximum_fusion.5), channel_id=1, source_target_pairs={{4,0},{8,4},{12,8},{16,12},{20,16},{24,20},{28,24},{5,1},{9,5},{13... | collective-permute-start | bytes 4718600 | tf_op jit(solution)/shard_map/ppermute | solution.py:248
  106.9 3.9 %copy-start.13 = (bf16[384,4,256]{2,0,1:T(8,128)(2,1)}, bf16[384,4,256]{2,0,1:T(8,128)(2,1)S(1)}, u32[]{:S(2)}) copy-start(bf16[384,4,256]{2,0,1:T(8,128)(2,1)S(1)} %all-to-all-done.2) | copy-start | bytes 2359300
  106.9 61.0 %all-to-all-start.4 = ((bf16[384,4,256]{2,0,1:T(8,128)(2,1)}), bf16[384,4,256]{2,0,1:T(8,128)(2,1)S(1)}, u32[]{:S(2)}, u32[]{:S(2)}) async-start(bf16[384,4,256]{2,0,1:T(8,128)(2,1)} %copy.16), calls=%async_computation.4 | async-start | bytes 1572864 | tf_op jit(solution)/shard_map/all_to_all | solution.py:207
  156.6 99.0 %collective-permute-start.8 = (bf16[4,384,512]{2,1,0:T(8,128)(2,1)}, bf16[4,384,512]{2,1,0:T(8,128)(2,1)}, u32[]{:S(2)}, u32[]{:S(2)}) collective-permute-start(bf16[4,384,512]{2,1,0:T(8,128)(2,1)} %get-tuple-element.44), channel_id=1, source_target_pairs={{4,0},{8,4},{12,8},{16,12},{20,16},{24,20},{28,24},{5,1},{9,5},{13... | collective-permute-start | bytes 4718600 | tf_op jit(solution)/shard_map/ppermute | solution.py:260
  167.9 6.0 %copy-start.14 = (bf16[384,4,256]{2,0,1:T(8,128)(2,1)}, bf16[384,4,256]{2,0,1:T(8,128)(2,1)S(1)}, u32[]{:S(2)}) copy-start(bf16[384,4,256]{2,0,1:T(8,128)(2,1)S(1)} %all-to-all-done.4) | copy-start | bytes 2359300
  168.0 66.8 %all-to-all-start.1 = ((bf16[4,384,256]{2,1,0:T(8,128)(2,1)}), bf16[4,384,256]{2,1,0:T(8,128)(2,1)S(1)}, u32[]{:S(2)}, u32[]{:S(2)}) async-start(bf16[4,384,256]{2,1,0:T(8,128)(2,1)} %bitcast.4), calls=%async_computation.1 | async-start | bytes 1572864 | tf_op jit(solution)/shard_map/all_to_all | solution.py:211
  171.9 83.7 %collective-permute-start.9 = (bf16[4,384,512]{2,1,0:T(8,128)(2,1)}, bf16[4,384,512]{2,1,0:T(8,128)(2,1)}, u32[]{:S(2)}, u32[]{:S(2)}) collective-permute-start(bf16[4,384,512]{2,1,0:T(8,128)(2,1)} %get-tuple-element.45), channel_id=1, source_target_pairs={{0,4},{4,8},{8,12},{12,16},{16,20},{20,24},{24,28},{1,5},{5,9},{9,... | collective-permute-start | bytes 4718600 | tf_op jit(solution)/shard_map/ppermute | solution.py:261
  219.7 44.7 %collective-permute-start.10 = (bf16[4,384,512]{2,1,0:T(8,128)(2,1)}, bf16[4,384,512]{2,1,0:T(8,128)(2,1)}, u32[]{:S(2)}, u32[]{:S(2)}) collective-permute-start(bf16[4,384,512]{2,1,0:T(8,128)(2,1)} %get-tuple-element.47), channel_id=1, source_target_pairs={{4,0},{8,4},{12,8},{16,12},{20,16},{24,20},{28,24},{5,1},{9,5},{13... | collective-permute-start | bytes 4718600 | tf_op jit(solution)/shard_map/ppermute | solution.py:260
  232.9 31.5 %collective-permute-start.11 = (bf16[4,384,512]{2,1,0:T(8,128)(2,1)}, bf16[4,384,512]{2,1,0:T(8,128)(2,1)}, u32[]{:S(2)}, u32[]{:S(2)}) collective-permute-start(bf16[4,384,512]{2,1,0:T(8,128)(2,1)} %get-tuple-element.48), channel_id=1, source_target_pairs={{0,4},{4,8},{8,12},{12,16},{16,20},{20,24},{24,28},{1,5},{5,9},{9,... | collective-permute-start | bytes 4718600 | tf_op jit(solution)/shard_map/ppermute | solution.py:261
  234.8 13.9 %all-to-all-start.3 = ((bf16[4,384,256]{2,1,0:T(8,128)(2,1)}), bf16[4,384,256]{2,1,0:T(8,128)(2,1)S(1)}, u32[]{:S(2)}, u32[]{:S(2)}) async-start(bf16[4,384,256]{2,1,0:T(8,128)(2,1)} %bitcast.8), calls=%async_computation.3 | async-start | bytes 1572864 | tf_op jit(solution)/shard_map/all_to_all | solution.py:211
  248.7 13.7 %all-to-all-start.5 = ((bf16[4,384,256]{2,1,0:T(8,128)(2,1)}), bf16[4,384,256]{2,1,0:T(8,128)(2,1)S(1)}, u32[]{:S(2)}, u32[]{:S(2)}) async-start(bf16[4,384,256]{2,1,0:T(8,128)(2,1)} %bitcast.45), calls=%async_computation.5 | async-start | bytes 1572864 | tf_op jit(solution)/shard_map/all_to_all | solution.py:211
  252.2 3.3 %copy-start.8 = (f32[4,384,256]{2,1,0:T(8,128)S(1)}, f32[4,384,256]{2,1,0:T(8,128)}, u32[]{:S(2)}) copy-start(f32[4,384,256]{2,1,0:T(8,128)} %get-tuple-element.43) | copy-start | bytes 4718596
  252.2 3.3 %copy-start.9 = (f32[4,384,256]{2,1,0:T(8,128)S(1)}, f32[4,384,256]{2,1,0:T(8,128)}, u32[]{:S(2)}) copy-start(f32[4,384,256]{2,1,0:T(8,128)} %get-tuple-element.50) | copy-start | bytes 4718596
  262.6 1.8 copy-start.10
  262.6 2.7 %copy-start.11 = (f32[4,384,256]{2,1,0:T(8,128)S(1)}, f32[4,384,256]{2,1,0:T(8,128)}, u32[]{:S(2)}) copy-start(f32[4,384,256]{2,1,0:T(8,128)} %get-tuple-element.51) | copy-start | bytes 4718596
  265.4 2.5 copy-start.5
  265.4 2.5 copy-start.7
  267.9 1.6 copy-start.6

commit v2 on v1

v2 whole, which is shorter than its diff:
```python
import functools
import math

import jax
import jax.numpy as jnp
from jax import lax
from jax.experimental import pallas as pl
from jax.experimental.pallas import tpu as pltpu
from jax.sharding import PartitionSpec as P

HD = 128
TILE = 384
SPT = 4
KSLOT = 8
SCALE = 1.0 / math.sqrt(HD)
EXP2_SCALE = SCALE * math.log2(math.e)


def dot_nn(a, b):
    return lax.dot_general(a, b, (((1,), (0,)), ((), ())), preferred_element_type=jnp.float32)


def dot_nt(a, b):
    return lax.dot_general(a, b, (((1,), (1,)), ((), ())), preferred_element_type=jnp.float32)


def fold_rows(block, op):
    return op(block.reshape(TILE // 8, 8, TILE), axis=0)


def load_extended(heads, own_tiles, first_col, rim_first, rim_width, k_hbm, v_hbm, low_hbm,
                  high_hbm, kext, vext, sems):
    width = heads * HD
    copies = []
    for n, (dst, own_src) in enumerate(((kext, k_hbm), (vext, v_hbm))):
        rim = pl.ds(n * rim_width + rim_first, width)
        own = pl.ds(first_col, width)
        copies.append(pltpu.make_async_copy(
            low_hbm.at[:, :, rim], dst.at[pl.ds(0, SPT)], sems.at[3 * n]))
        copies.append(pltpu.make_async_copy(
            own_src.at[:, :, own], dst.at[pl.ds(SPT, own_tiles)], sems.at[3 * n + 1]))
        copies.append(pltpu.make_async_copy(
            high_hbm.at[:, :, rim], dst.at[pl.ds(SPT + own_tiles, SPT)], sems.at[3 * n + 2]))
    return copies


def attention_kernel(heads, own_tiles, first_col, rim_in, rim_out, aliased, *refs):
    idx_ref, cnt_ref, q_ref, do_ref, k_hbm, v_hbm, low_hbm, high_hbm = refs[:8]
    refs = refs[8 + aliased:]
    o_ref, dq_ref, dk_own, dv_own, low_out, high_out = refs[:6]
    kext, vext, dk, dv, sems = refs[6:11]
    per_head = [refs[11 + 6 * h:17 + 6 * h] for h in range(heads)]
    kt, vt, scores, tops_at, o_acc, dq_acc = zip(*per_head)
    a = pl.program_id(0)
    ext_tiles = own_tiles + 2 * SPT
    width = heads * HD
    cols = [slice(h * HD, (h + 1) * HD) for h in range(heads)]

    @pl.when(a == 0)
    def _():
        copies = load_extended(heads, own_tiles, first_col, *rim_in, k_hbm, v_hbm, low_hbm,
                               high_hbm, kext, vext, sems)
        for copy in copies:
            copy.start()
        dk[...] = jnp.zeros_like(dk)
        dv[...] = jnp.zeros_like(dv)
        for copy in copies:
            copy.wait()

        @pl.loop(0, ext_tiles)
        def _(t):
            for h in range(heads):
                kt[h][t] = kext[t, :, cols[h]].T
                vt[h][t] = vext[t, :, cols[h]].T

    count = cnt_ref[a]

    def score_slot(s, carry):
        t = idx_ref[a * KSLOT + s]
        new = []
        blocks = [dot_nt(kext[t, :, cols[h]], q_ref[:, cols[h]]) for h in range(heads)]
        for h in range(heads):
            old, total = carry[h]
            top = jnp.maximum(old, jnp.max(fold_rows(blocks[h], jnp.max), axis=0, keepdims=True))
            weights = jnp.exp2((blocks[h] - top) * EXP2_SCALE)
            scores[h][s] = weights
            tops_at[h][s] = top
            total = total * jnp.exp2((old - top) * EXP2_SCALE) + fold_rows(weights, jnp.sum)
            new.append((top, total))
        return tuple(new)

    start = (jnp.full((1, TILE), -jnp.inf, jnp.float32), jnp.zeros((8, TILE), jnp.float32))
    stats = lax.fori_loop(0, count, score_slot, (start,) * heads)
    tops = [top for top, _ in stats]
    inverse = [1.0 / jnp.sum(total, axis=0, keepdims=True) for _, total in stats]
    for h in range(heads):
        o_acc[h][...] = jnp.zeros_like(o_acc[h])
        dq_acc[h][...] = jnp.zeros_like(dq_acc[h])

    def weights_of(h, s):
        factor = jnp.exp2((tops_at[h][s] - tops[h]) * EXP2_SCALE) * inverse[h]
        return scores[h][s] * factor

    @pl.loop(0, count)
    def _(s):
        t = idx_ref[a * KSLOT + s]
        lows = [weights_of(h, s).astype(jnp.bfloat16) for h in range(heads)]
        outs = [dot_nn(vt[h][t], lows[h]) for h in range(heads)]
        terms = [dot_nn(lows[h], do_ref[:, cols[h]]) for h in range(heads)]
        for h in range(heads):
            o_acc[h][...] += outs[h]
        dv[t] += jnp.concatenate(terms, axis=1)

    deltas = []
    for h in range(heads):
        out_t = o_acc[h][...].astype(jnp.bfloat16).astype(jnp.float32)
        grads_t = do_ref[:, cols[h]].astype(jnp.float32).T
        deltas.append(jnp.sum(out_t * grads_t, axis=0, keepdims=True))
        o_ref[:, cols[h]] = out_t.T.astype(jnp.bfloat16)

    @pl.loop(0, count)
    def _(s):
        t = idx_ref[a * KSLOT + s]
        grads = [dot_nt(vext[t, :, cols[h]], do_ref[:, cols[h]]) for h in range(heads)]
        lows = [
            (weights_of(h, s) * (grads[h] - deltas[h])).astype(jnp.bfloat16) for h in range(heads)
        ]
        terms = [dot_nn(lows[h], q_ref[:, cols[h]]) for h in range(heads)]
        query_terms = [dot_nn(kt[h][t], lows[h]) for h in range(heads)]
        dk[t] += jnp.concatenate(terms, axis=1)
        for h in range(heads):
            dq_acc[h][...] += query_terms[h]

    for h in range(heads):
        dq_ref[:, cols[h]] = (dq_acc[h][...] * SCALE).T.astype(jnp.bfloat16)

    @pl.when(a == own_tiles - 1)
    def _():
        own = pl.ds(SPT, own_tiles)
        rim_first, rim_width = rim_out

        @pl.loop(0, ext_tiles)
        def _(t):
            scaled = dk[t] * SCALE
            dk[t] = scaled
            kext[t] = scaled.astype(jnp.bfloat16)
            vext[t] = dv[t].astype(jnp.bfloat16)

        copies = []
        for n, (src, wide, own_dst) in enumerate(((kext, dk, dk_own), (vext, dv, dv_own))):
            rim = pl.ds(n * rim_width + rim_first, width)
            copies.append(pltpu.make_async_copy(
                src.at[pl.ds(0, SPT)], low_out.at[:, :, rim], sems.at[3 * n]))
            copies.append(pltpu.make_async_copy(
                wide.at[own], own_dst.at[:, :, pl.ds(rim_first, width)], sems.at[3 * n + 1]))
            copies.append(pltpu.make_async_copy(
                src.at[pl.ds(SPT + own_tiles, SPT)], high_out.at[:, :, rim], sems.at[3 * n + 2]))
        for copy in copies:
            copy.start()
        for copy in copies:
            copy.wait()


def attention(heads, first, in_span, out_span, idx, cnt, queries, grads, keys, values, low, high,
              dq_before, out_before):
    rows, all_cols = queries.shape
    own_tiles = rows // TILE
    ext_tiles = own_tiles + 2 * SPT
    width = heads * HD
    col_block = first // heads
    in_block = (first - in_span[0]) // heads
    out_block = (first - out_span[0]) // heads
    in_width, out_width = in_span[1] * HD, out_span[1] * HD
    smem = pl.BlockSpec(memory_space=pltpu.SMEM)
    hbm = pl.BlockSpec(memory_space=pl.ANY)
    rim = jax.ShapeDtypeStruct((SPT, TILE, 2 * out_width), jnp.bfloat16)
    own = jax.ShapeDtypeStruct((own_tiles, TILE, out_width), jnp.float32)
    out_shape = [
        jax.ShapeDtypeStruct((rows, out_width), jnp.bfloat16),
        jax.ShapeDtypeStruct((rows, all_cols), jnp.bfloat16),
        own, own, rim, rim,
    ]
    before, aliases = [], {}
    if dq_before is not None:
        aliases[8 + len(before)] = 1
        before.append(dq_before)
    if out_before is not None:
        for at, array in zip((0, 2, 3, 4, 5), out_before):
            aliases[8 + len(before)] = at
            before.append(array)
    pairs = own_tiles * 6 * heads
    per_head = [
        pltpu.VMEM((ext_tiles, HD, TILE), jnp.bfloat16),
        pltpu.VMEM((ext_tiles, HD, TILE), jnp.bfloat16),
        pltpu.VMEM((KSLOT, TILE, TILE), jnp.float32),
        pltpu.VMEM((KSLOT, 1, TILE), jnp.float32),
        pltpu.VMEM((HD, TILE), jnp.float32),
        pltpu.VMEM((HD, TILE), jnp.float32),
    ]
    out, dq, *rest = pl.pallas_call(
        functools.partial(
            attention_kernel, heads, own_tiles, first * HD,
            ((first - in_span[0]) * HD, in_width), ((first - out_span[0]) * HD, out_width),
            len(before),
        ),
        grid=(own_tiles,),
        in_specs=[
            smem, smem,
            pl.BlockSpec((TILE, width), lambda a: (a, col_block)),
            pl.BlockSpec((TILE, width), lambda a: (a, in_block)),
            hbm, hbm, hbm, hbm,
        ] + [hbm] * len(before),
        out_specs=[
            pl.BlockSpec((TILE, width), lambda a: (a, out_block)),
            pl.BlockSpec((TILE, width), lambda a: (a, col_block)),
            hbm, hbm, hbm, hbm,
        ],
        out_shape=out_shape,
        input_output_aliases=aliases,
        scratch_shapes=[
            pltpu.VMEM((ext_tiles, TILE, width), jnp.bfloat16),
            pltpu.VMEM((ext_tiles, TILE, width), jnp.bfloat16),
            pltpu.VMEM((ext_tiles, TILE, width), jnp.float32),
            pltpu.VMEM((ext_tiles, TILE, width), jnp.float32),
            pltpu.SemaphoreType.DMA((6,)),
        ] + per_head * heads,
        compiler_params=pltpu.CompilerParams(vmem_limit_bytes=56 * 1024 * 1024),
        cost_estimate=pl.CostEstimate(
            flops=pairs * 30 * TILE * TILE * HD,
            bytes_accessed=30 * rows * width,
            transcendentals=pairs * TILE * TILE,
        ),
    )(idx, cnt, queries, grads, keys, values, low, high, *before)
    return dq, (out, *rest)


def finish_kernel(own_tiles, k_own, v_own, ka, va, kb, vb, *refs):
    dk_ref, dv_ref = refs[-2:]
    a = pl.program_id(0)
    above = jnp.where(a >= own_tiles - SPT, 1.0, 0.0)
    below = jnp.where(a < SPT, 1.0, 0.0)
    for own, hi, lo, out in ((k_own, ka, kb, dk_ref), (v_own, va, vb, dv_ref)):
        total = own[0] + above * hi[0].astype(jnp.float32) + below * lo[0].astype(jnp.float32)
        out[...] = total.astype(jnp.bfloat16)


def finish(span, all_cols, dk_own, dv_own, from_above, from_below, before):
    own_tiles = dk_own.shape[0]
    width = span[1] * HD
    col_block = span[0] // span[1]
    own = pl.BlockSpec((1, TILE, width), lambda a: (a, 0, 0))

    def rim(shift, part):
        return pl.BlockSpec(
            (1, TILE, width), lambda a: (jnp.clip(a - shift, 0, SPT - 1), 0, part))

    out = pl.BlockSpec((TILE, width), lambda a: (a, col_block))
    shape = jax.ShapeDtypeStruct((own_tiles * TILE, all_cols), jnp.bfloat16)
    gap = own_tiles - SPT
    return pl.pallas_call(
        functools.partial(finish_kernel, own_tiles),
        grid=(own_tiles,),
        in_specs=[own, own, rim(gap, 0), rim(gap, 1), rim(0, 0), rim(0, 1)]
        + [pl.BlockSpec(memory_space=pl.ANY)] * len(before),
        out_specs=[out, out],
        out_shape=[shape, shape],
        input_output_aliases={6 + n: n for n in range(len(before))},
        compiler_params=pltpu.CompilerParams(vmem_limit_bytes=32 * 1024 * 1024),
        cost_estimate=pl.CostEstimate(
            flops=4 * own_tiles * TILE * width,
            bytes_accessed=20 * own_tiles * TILE * width,
            transcendentals=0,
        ),
    )(dk_own, dv_own, from_above, from_above, from_below, from_below, *before)


def neighbours(axis):
    count = lax.axis_size(axis)
    up = [(i, i + 1) for i in range(count - 1)]
    return up, [(b, a) for a, b in up]


def scatter_heads(block):
    return lax.all_to_all(block, "head", split_axis=1, concat_axis=0, tiled=True)


def gather_heads(block):
    return lax.all_to_all(block, "head", split_axis=0, concat_axis=1, tiled=True)


def head_plan(heads_here):
    size = 2
    groups = [(at, min(size, heads_here - at)) for at in range(0, heads_here, size)]
    first, last = groups[0], groups[-1]
    in_spans, out_spans = [first], [(0, last[0]), last]
    if heads_here > first[1]:
        in_spans.append((first[1], heads_here - first[1]))
    else:
        out_spans = [last]
    return groups, in_spans, out_spans


def span_of(head, spans):
    return [n for n, (at, count) in enumerate(spans) if at <= head < at + count][0]


def shards(queries, key_states, value_states, out_grads, pattern):
    row_count, col_count = queries.shape
    own_tiles = row_count // TILE
    head_devices = lax.axis_size("head")
    own_rows = out_grads.shape[0]
    first_tile = lax.axis_index("ctx") * own_tiles
    listed = lax.dynamic_slice_in_dim(pattern, first_tile, own_tiles, 0)
    allowed = listed >= 0
    idx = jnp.where(allowed, listed - (first_tile - SPT), 0).reshape(-1).astype(jnp.int32)
    cnt = jnp.sum(allowed.astype(jnp.int32), axis=1)
    up, down = neighbours("ctx")
    groups, in_spans, out_spans = head_plan(col_count // HD)
    keys_tiled = key_states.reshape(own_tiles, TILE, col_count)
    values_tiled = value_states.reshape(own_tiles, TILE, col_count)
    by_head = out_grads.reshape(own_rows, head_devices, col_count)

    lows, highs, grads = [], [], []
    for at, heads in in_spans:
        cols = slice(at * HD, (at + heads) * HD)
        packed = jnp.concatenate((keys_tiled[:, :, cols], values_tiled[:, :, cols]), axis=2)
        grad_part = by_head[:, :, cols]
        if lows:
            packed, grad_part, lows[-1], highs[-1], grads[-1] = lax.optimization_barrier(
                (packed, grad_part, lows[-1], highs[-1], grads[-1]))
        lows.append(lax.ppermute(packed[own_tiles - SPT:], "ctx", up))
        highs.append(lax.ppermute(packed[:SPT], "ctx", down))
        grads.append(scatter_heads(grad_part.reshape(own_rows, -1)))

    dq, parts = None, [None] * len(out_spans)
    for at, heads in groups:
        source, target = span_of(at, in_spans), span_of(at, out_spans)
        dq, parts[target] = attention(
            heads, at, in_spans[source], out_spans[target], idx, cnt, queries, grads[source],
            keys_tiled, values_tiled, lows[source], highs[source], dq, parts[target],
        )

    attended, sums = [], ()
    for span, (out, dk_own, dv_own, low, high) in zip(out_spans, parts):
        attended.append(gather_heads(out).reshape(own_rows, head_devices, span[1] * HD))
        from_above = lax.ppermute(low, "ctx", down)
        from_below = lax.ppermute(high, "ctx", up)
        sums = finish(span, col_count, dk_own, dv_own, from_above, from_below, sums)
    attended = jnp.concatenate(attended, axis=2).reshape(own_rows, head_devices * col_count)
    return attended, dq, sums[0], sums[1]


def solution(mesh):
    return jax.shard_map(
        shards,
        mesh=mesh,
        in_specs=(
            P("ctx", "head"),
            P("ctx", "head"),
            P("ctx", "head"),
            P(("ctx", "head"), None),
            P(),
        ),
        out_specs=(P(("ctx", "head"), None), P("ctx", "head"), P("ctx", "head"), P("ctx", "head")),
        check_vma=False,
    )
```

time: 276 us -> 257 us (0.931)
  the two profiles are of different devices: /device:TPU:1 before, /device:TPU:24 now
where the time goes in v2:
time: 257 us; the launch traced here: 254 us
  Pallas kernels  155 us (60%)
  starting transfers between devices  49.5 us (19%)
  blocking collectives  23.1 us (9%)
  local copies, waits for them, and re-layouts  16 us (6%)
  waiting for transfers between devices  6.07 us (2%)
  other arithmetic  3.77 us (1%)
    pallas_call x3, Pallas kernels, attention(): pl.pallas_call(functools.partial(attention_kernel, heads, own_tiles, firs...  146 us
    all_to_all x1, blocking collectives, gather_heads(): lax.all_to_all(block, 'head', split_axis=0, concat_axis=1, tiled=True)  23.1 us
    ppermute x2, starting transfers between devices, shards(): from_below = lax.ppermute(high, 'ctx', up)  15.3 us
    ppermute x2, starting transfers between devices, shards(): from_above = lax.ppermute(low, 'ctx', down)  9.92 us
    pallas_call x2, Pallas kernels, finish(): pl.pallas_call(functools.partial(finish_kernel, own_tiles), grid=(own_til...  8.95 us
    all_to_all x2, starting transfers between devices, scatter_heads(): lax.all_to_all(block, 'head', split_axis=1, concat_axis=0, tiled=True)  8.56 us
    ppermute x2, starting transfers between devices, shards(): lows.append(lax.ppermute(packed[own_tiles - SPT:], 'ctx', up))  7.39 us
    all_to_all x2, waiting for transfers between devices, scatter_heads(): lax.all_to_all(block, 'head', split_axis=1, concat_axis=0, tiled=True)  6.05 us
  transfers between devices with their start and end apart: 11, of which 1 were waited for; matrix products, arithmetic and copies ran while one was open for 6% of the time, Pallas kernels for 40%

profile of v2, /device:TPU:24, one launch (start us, length us, event | category | flops | bytes accessed | tf_op | source)
XLA Modules:
  0.0 254.1 jit_solution(651878991152804971)
XLA Ops:
  0.6 1.2 slice.27
  1.8 1.2 slice.28
  3.0 1.3 pad_maximum_fusion.1
  4.3 1.9 collective-permute-start.1
  6.2 3.6 %collective-permute-start = (bf16[4,384,512]{2,1,0:T(8,128)(2,1)}, bf16[4,384,512]{2,1,0:T(8,128)(2,1)}, u32[]{:S(2)}, u32[]{:S(2)}) collective-permute-start(bf16[4,384,512]{2,1,0:T(8,128)(2,1)} %pad_maximum_fusion.1), channel_id=1, source_target_pairs={{0,4},{4,8},{8,12},{12,16},{16,20},{20,24},{24,28},{1,5},{5,9},{9,... | collective-permute-start | bytes 4718600 | tf_op jit(solution)/shard_map/ppermute | solution.py:331
  9.8 4.5 %reshape.46 = bf16[384,4,768]{2,1,0:T(4,128)(2,1)S(1)} reshape(bf16[384,3072]{1,0:T(8,128)(2,1)} %param.8) | data formatting | bytes 4718592 | tf_op jit(solution)/shard_map/reshape | solution.py:321
  14.4 0.3 slice.29
  14.7 1.0 copy.23
  15.7 4.2 %all-to-all-start = ((bf16[384,4,256]{2,0,1:T(8,128)(2,1)}), bf16[384,4,256]{2,0,1:T(8,128)(2,1)}, u32[]{:S(2)}, u32[]{:S(2)}) async-start(bf16[384,4,256]{2,0,1:T(8,128)(2,1)} %copy.23), calls=%async_computation | async-start | bytes 1572864 | tf_op jit(solution)/shard_map/all_to_all | solution.py:284
  19.9 0.0 copy-start.4
  19.9 1.7 slice.24
  21.5 0.5 copy-done.4
  22.0 0.1 slice.25
  22.1 0.5 slice.26
  22.7 1.4 copy.22
  24.1 0.0 copy-start.5
  24.1 0.4 pad_maximum_fusion
  24.5 6.0 %all-to-all-done = bf16[384,4,256]{2,0,1:T(8,128)(2,1)} async-done(((bf16[384,4,256]{2,0,1:T(8,128)(2,1)}), bf16[384,4,256]{2,0,1:T(8,128)(2,1)}, u32[]{:S(2)}, u32[]{:S(2)}) %all-to-all-start) | async-done | bytes 786464 | tf_op jit(solution)/shard_map/all_to_all | solution.py:284
  30.6 0.0 collective-permute-done.1.refs_7_
  30.6 0.0 collective-permute-done.refs_6_
  30.6 2.2 collective-permute-start.3
  32.8 3.8 %collective-permute-start.2 = (bf16[4,384,1024]{2,1,0:T(8,128)(2,1)S(1)}, bf16[4,384,1024]{2,1,0:T(8,128)(2,1)}, u32[]{:S(2)}, u32[]{:S(2)}) collective-permute-start(bf16[4,384,1024]{2,1,0:T(8,128)(2,1)S(1)} %pad_maximum_fusion), channel_id=1, source_target_pairs={{0,4},{4,8},{8,12},{12,16},{16,20},{20,24},{24,28},{1,5},{5,9},{9,... | collective-permute-start | bytes 9437192 | tf_op jit(solution)/shard_map/ppermute | solution.py:331
  36.6 0.0 copy-done.5
  36.6 0.6 convert_reduce_fusion
  37.2 0.1 subtract_select_fusion
  37.3 0.1 copy.18
  37.3 0.6 reshape.43.refs_0_
  37.9 4.4 %all-to-all-start.1 = ((bf16[384,4,512]{2,0,1:T(8,128)(2,1)}), bf16[384,4,512]{2,0,1:T(8,128)(2,1)}, u32[]{:S(2)}, u32[]{:S(2)}) async-start(bf16[384,4,512]{2,0,1:T(8,128)(2,1)} %copy.22), calls=%async_computation.1 | async-start | bytes 3145728 | tf_op jit(solution)/shard_map/all_to_all | solution.py:284
  42.3 48.6 %shard_map.84 = (bf16[1536,512]{1,0:T(8,128)(2,1)}, bf16[1536,768]{1,0:T(8,128)(2,1)}, f32[4,384,512]{2,1,0:T(8,128)}, f32[4,384,512]{2,1,0:T(8,128)}, bf16[4,38...) custom-call(s32[32]{0:T(128)} %reshape.43.refs_0_, s32[4]{0:T(128)} %get-tuple-element.58.refs_1_, ...), custom_call_target="tpu_custom_call" | custom-call | flops 27179089920 | bytes 11796480 | tf_op jit(solution)/shard_map/pallas_call | solution.py:200
  91.0 0.0 all-to-all-done.1
  91.0 0.0 collective-permute-done.3.refs_7_
  91.0 0.0 collective-permute-done.2.refs_6_
  91.0 48.6 %shard_map.85 = (bf16[1536,512]{1,0:T(8,128)(2,1)}, bf16[1536,768]{1,0:T(8,128)(2,1)}, f32[4,384,512]{2,1,0:T(8,128)}, f32[4,384,512]{2,1,0:T(8,128)}, bf16[4,38...) custom-call(s32[32]{0:T(128)} %reshape.43.refs_0_, ...), custom_call_target="tpu_custom_call", output_to_operand_aliasing={{1}: (8, {}), {0}: (9, {}), {2}: (10, {}), {3}: (11, {}), {... | custom-call | flops 27179089920 | bytes 11796480 | tf_op jit(solution)/shard_map/pallas_call | solution.py:200
  139.6 8.0 %collective-permute-start.6 = (bf16[4,384,1024]{2,1,0:T(8,128)(2,1)}, bf16[4,384,1024]{2,1,0:T(8,128)(2,1)S(1)}, u32[]{:S(2)}, u32[]{:S(2)}) collective-permute-start(bf16[4,384,1024]{2,1,0:T(8,128)(2,1)} %get-tuple-element.52), channel_id=1, source_target_pairs={{4,0},{8,4},{12,8},{16,12},{20,16},{24,20},{28,24},{5,1},{9,5},{13... | collective-permute-start | bytes 9437192 | tf_op jit(solution)/shard_map/ppermute | solution.py:346
  147.6 7.2 %collective-permute-start.7 = (bf16[4,384,1024]{2,1,0:T(8,128)(2,1)}, bf16[4,384,1024]{2,1,0:T(8,128)(2,1)}, u32[]{:S(2)}, u32[]{:S(2)}) collective-permute-start(bf16[4,384,1024]{2,1,0:T(8,128)(2,1)} %get-tuple-element.53), channel_id=1, source_target_pairs={{0,4},{4,8},{8,12},{12,16},{16,20},{20,24},{24,28},{1,5},{5,9},{9,... | collective-permute-start | bytes 9437192 | tf_op jit(solution)/shard_map/ppermute | solution.py:347
  154.9 48.5 %shard_map.86 = (bf16[1536,256]{1,0:T(8,128)(2,1)}, bf16[1536,768]{1,0:T(8,128)(2,1)}, f32[4,384,256]{2,1,0:T(8,128)}, f32[4,384,256]{2,1,0:T(8,128)}, bf16[4,38...) custom-call(s32[32]{0:T(128)} %reshape.43.refs_0_, ...), custom_call_target="tpu_custom_call", output_to_operand_aliasing={{1}: (8, {})} | custom-call | flops 27179089920 | bytes 11796480 | tf_op jit(solution)/shard_map/pallas_call | solution.py:200
  203.4 4.2 %all-to-all-start.3 = ((bf16[4,384,256]{2,1,0:T(8,128)(2,1)}), bf16[4,384,256]{2,1,0:T(8,128)(2,1)}, u32[]{:S(2)}, u32[]{:S(2)}) async-start(bf16[4,384,256]{2,1,0:T(8,128)(2,1)} %bitcast.28), calls=%async_computation.3 | async-start | bytes 1572864 | tf_op jit(solution)/shard_map/all_to_all | solution.py:288
  207.6 1.9 collective-permute-start.4
  209.5 8.1 %collective-permute-start.5 = (bf16[4,384,512]{2,1,0:T(8,128)(2,1)}, bf16[4,384,512]{2,1,0:T(8,128)(2,1)}, u32[]{:S(2)}, u32[]{:S(2)}) collective-permute-start(bf16[4,384,512]{2,1,0:T(8,128)(2,1)} %get-tuple-element.49), channel_id=1, source_target_pairs={{0,4},{4,8},{8,12},{12,16},{16,20},{20,24},{24,28},{1,5},{5,9},{9,... | collective-permute-start | bytes 4718600 | tf_op jit(solution)/shard_map/ppermute | solution.py:347
  217.6 0.0 all-to-all-done.3
  217.6 23.1 %all_to_all.64 = bf16[4,384,512]{2,1,0:T(8,128)(2,1)S(1)} all-to-all(bf16[4,384,512]{2,1,0:T(8,128)(2,1)} %bitcast.27), channel_id=1, replica_groups=mesh['ctx'=8,'head'=4] {'head'}, dimensions={0} | all-to-all | bytes 3145728 | tf_op jit(solution)/shard_map/all_to_all | solution.py:288
  240.7 0.0 copy-start.1
  240.7 1.4 maximum_bitcast_fusion
  242.2 0.0 copy-start
  242.2 1.7 copy.24
  243.9 0.0 collective-permute-done.6.ka.va
  243.9 0.0 collective-permute-done.7.kb.vb
  243.9 0.0 copy-done.1
  243.9 1.2 copy-done
  245.1 0.0 copy-start.2
  245.1 0.0 copy-start.3
  245.1 4.8 %shard_map.87 = (bf16[1536,768]{1,0:T(8,128)(2,1)}, bf16[1536,768]{1,0:T(8,128)(2,1)}) custom-call(f32[4,384,512]{2,1,0:T(8,128)S(1)} %copy-done, f32[4,384,512]{2,1,0:T(8,128)S(1)} %copy-done.1, bf16[4,384,1024]{2,1,0:T(8,128)(2,1)S(1)} %collective-permute-done.6.ka.va, bf16[4,384,1024]{2,1,0:T(8,128)(2,1)S(1)} %collective-permute-done.6.ka.va, ...), custom_call_target="tpu_custom_call" | custom-call | flops 3145728 | bytes 15728640 | tf_op jit(solution)/shard_map/pallas_call | solution.py:260
  249.9 0.0 collective-permute-done.4.ka.va
  249.9 0.0 collective-permute-done.5.kb.vb
  249.9 0.0 copy-done.2
  249.9 0.0 copy-done.3
  250.0 4.1 %shard_map.88 = (bf16[1536,768]{1,0:T(8,128)(2,1)}, bf16[1536,768]{1,0:T(8,128)(2,1)}) custom-call(f32[4,384,256]{2,1,0:T(8,128)S(1)} %copy-done.2, f32[4,384,256]{2,1,0:T(8,128)S(1)} %copy-done.3, bf16[4,384,512]{2,1,0:T(8,128)(2,1)} %collective-permute-done.4.ka.va, ...), custom_call_target="tpu_custom_call", output_to_operand_aliasing={{0}: (6, {}), {1}: (7, {})} | custom-call | flops 1572864 | bytes 7864320 | tf_op jit(solution)/shard_map/pallas_call | solution.py:260
Async XLA Ops:
  4.3 26.3 %collective-permute-start.1 = (bf16[4,384,512]{2,1,0:T(8,128)(2,1)}, bf16[4,384,512]{2,1,0:T(8,128)(2,1)}, u32[]{:S(2)}, u32[]{:S(2)}) collective-permute-start(bf16[4,384,512]{2,1,0:T(8,128)(2,1)} %pad_maximum_fusion.1), channel_id=1, source_target_pairs={{4,0},{8,4},{12,8},{16,12},{20,16},{24,20},{28,24},{5,1},{9,5},{13... | collective-permute-start | bytes 4718600 | tf_op jit(solution)/shard_map/ppermute | solution.py:332
  6.2 24.4 %collective-permute-start = (bf16[4,384,512]{2,1,0:T(8,128)(2,1)}, bf16[4,384,512]{2,1,0:T(8,128)(2,1)}, u32[]{:S(2)}, u32[]{:S(2)}) collective-permute-start(bf16[4,384,512]{2,1,0:T(8,128)(2,1)} %pad_maximum_fusion.1), channel_id=1, source_target_pairs={{0,4},{4,8},{8,12},{12,16},{16,20},{20,24},{24,28},{1,5},{5,9},{9,... | collective-permute-start | bytes 4718600 | tf_op jit(solution)/shard_map/ppermute | solution.py:331
  15.7 14.9 %all-to-all-start = ((bf16[384,4,256]{2,0,1:T(8,128)(2,1)}), bf16[384,4,256]{2,0,1:T(8,128)(2,1)}, u32[]{:S(2)}, u32[]{:S(2)}) async-start(bf16[384,4,256]{2,0,1:T(8,128)(2,1)} %copy.23), calls=%async_computation | async-start | bytes 1572864 | tf_op jit(solution)/shard_map/all_to_all | solution.py:284
  19.9 2.1 copy-start.4
  24.1 12.4 %copy-start.5 = (s32[32,8]{0,1:T(8,128)S(1)}, s32[32,8]{0,1:T(8,128)}, u32[]{:S(2)}) copy-start(s32[32,8]{0,1:T(8,128)} %param.9) | copy-start | bytes 3076
  30.6 60.4 %collective-permute-start.3 = (bf16[4,384,1024]{2,1,0:T(8,128)(2,1)S(1)}, bf16[4,384,1024]{2,1,0:T(8,128)(2,1)}, u32[]{:S(2)}, u32[]{:S(2)}) collective-permute-start(bf16[4,384,1024]{2,1,0:T(8,128)(2,1)S(1)} %pad_maximum_fusion), channel_id=1, source_target_pairs={{4,0},{8,4},{12,8},{16,12},{20,16},{24,20},{28,24},{5,1},{9,5},{13... | collective-permute-start | bytes 9437192 | tf_op jit(solution)/shard_map/ppermute | solution.py:332
  32.8 58.2 %collective-permute-start.2 = (bf16[4,384,1024]{2,1,0:T(8,128)(2,1)S(1)}, bf16[4,384,1024]{2,1,0:T(8,128)(2,1)}, u32[]{:S(2)}, u32[]{:S(2)}) collective-permute-start(bf16[4,384,1024]{2,1,0:T(8,128)(2,1)S(1)} %pad_maximum_fusion), channel_id=1, source_target_pairs={{0,4},{4,8},{8,12},{12,16},{16,20},{20,24},{24,28},{1,5},{5,9},{9,... | collective-permute-start | bytes 9437192 | tf_op jit(solution)/shard_map/ppermute | solution.py:331
  37.9 53.0 %all-to-all-start.1 = ((bf16[384,4,512]{2,0,1:T(8,128)(2,1)}), bf16[384,4,512]{2,0,1:T(8,128)(2,1)}, u32[]{:S(2)}, u32[]{:S(2)}) async-start(bf16[384,4,512]{2,0,1:T(8,128)(2,1)} %copy.22), calls=%async_computation.1 | async-start | bytes 3145728 | tf_op jit(solution)/shard_map/all_to_all | solution.py:284
  139.6 104.3 %collective-permute-start.6 = (bf16[4,384,1024]{2,1,0:T(8,128)(2,1)}, bf16[4,384,1024]{2,1,0:T(8,128)(2,1)S(1)}, u32[]{:S(2)}, u32[]{:S(2)}) collective-permute-start(bf16[4,384,1024]{2,1,0:T(8,128)(2,1)} %get-tuple-element.52), channel_id=1, source_target_pairs={{4,0},{8,4},{12,8},{16,12},{20,16},{24,20},{28,24},{5,1},{9,5},{13... | collective-permute-start | bytes 9437192 | tf_op jit(solution)/shard_map/ppermute | solution.py:346
  147.6 96.3 %collective-permute-start.7 = (bf16[4,384,1024]{2,1,0:T(8,128)(2,1)}, bf16[4,384,1024]{2,1,0:T(8,128)(2,1)}, u32[]{:S(2)}, u32[]{:S(2)}) collective-permute-start(bf16[4,384,1024]{2,1,0:T(8,128)(2,1)} %get-tuple-element.53), channel_id=1, source_target_pairs={{0,4},{4,8},{8,12},{12,16},{16,20},{20,24},{24,28},{1,5},{5,9},{9,... | collective-permute-start | bytes 9437192 | tf_op jit(solution)/shard_map/ppermute | solution.py:347
  203.4 14.2 %all-to-all-start.3 = ((bf16[4,384,256]{2,1,0:T(8,128)(2,1)}), bf16[4,384,256]{2,1,0:T(8,128)(2,1)}, u32[]{:S(2)}, u32[]{:S(2)}) async-start(bf16[4,384,256]{2,1,0:T(8,128)(2,1)} %bitcast.28), calls=%async_computation.3 | async-start | bytes 1572864 | tf_op jit(solution)/shard_map/all_to_all | solution.py:288
  207.6 42.3 %collective-permute-start.4 = (bf16[4,384,512]{2,1,0:T(8,128)(2,1)}, bf16[4,384,512]{2,1,0:T(8,128)(2,1)}, u32[]{:S(2)}, u32[]{:S(2)}) collective-permute-start(bf16[4,384,512]{2,1,0:T(8,128)(2,1)} %get-tuple-element.48), channel_id=1, source_target_pairs={{4,0},{8,4},{12,8},{16,12},{20,16},{24,20},{28,24},{5,1},{9,5},{13... | collective-permute-start | bytes 4718600 | tf_op jit(solution)/shard_map/ppermute | solution.py:346
  209.5 40.4 %collective-permute-start.5 = (bf16[4,384,512]{2,1,0:T(8,128)(2,1)}, bf16[4,384,512]{2,1,0:T(8,128)(2,1)}, u32[]{:S(2)}, u32[]{:S(2)}) collective-permute-start(bf16[4,384,512]{2,1,0:T(8,128)(2,1)} %get-tuple-element.49), channel_id=1, source_target_pairs={{0,4},{4,8},{8,12},{12,16},{16,20},{20,24},{24,28},{1,5},{5,9},{9,... | collective-permute-start | bytes 4718600 | tf_op jit(solution)/shard_map/ppermute | solution.py:347
  240.7 3.2 %copy-start.1 = (f32[4,384,512]{2,1,0:T(8,128)S(1)}, f32[4,384,512]{2,1,0:T(8,128)}, u32[]{:S(2)}) copy-start(f32[4,384,512]{2,1,0:T(8,128)} %get-tuple-element.51.v_own) | copy-start | bytes 9437188
  242.2 2.9 %copy-start = (f32[4,384,512]{2,1,0:T(8,128)S(1)}, f32[4,384,512]{2,1,0:T(8,128)}, u32[]{:S(2)}) copy-start(f32[4,384,512]{2,1,0:T(8,128)} %get-tuple-element.50.k_own) | copy-start | bytes 9437188
  245.1 4.9 %copy-start.2 = (f32[4,384,256]{2,1,0:T(8,128)S(1)}, f32[4,384,256]{2,1,0:T(8,128)}, u32[]{:S(2)}) copy-start(f32[4,384,256]{2,1,0:T(8,128)} %get-tuple-element.46.k_own) | copy-start | bytes 4718596
  245.1 4.9 %copy-start.3 = (f32[4,384,256]{2,1,0:T(8,128)S(1)}, f32[4,384,256]{2,1,0:T(8,128)}, u32[]{:S(2)}) copy-start(f32[4,384,256]{2,1,0:T(8,128)} %get-tuple-element.47.v_own) | copy-start | bytes 4718596

commit v3 on v2

--- a/solution.py
+++ b/solution.py
@@ -48,8 +48,8 @@
     idx_ref, cnt_ref, q_ref, do_ref, k_hbm, v_hbm, low_hbm, high_hbm = refs[:8]
     refs = refs[8 + aliased:]
     o_ref, dq_ref, dk_own, dv_own, low_out, high_out = refs[:6]
-    kext, vext, dk, dv, sems = refs[6:11]
-    per_head = [refs[11 + 6 * h:17 + 6 * h] for h in range(heads)]
+    kext, vext, dk, dv, q_wide, do_wide, sems = refs[6:13]
+    per_head = [refs[13 + 6 * h:19 + 6 * h] for h in range(heads)]
     kt, vt, scores, tops_at, o_acc, dq_acc = zip(*per_head)
     a = pl.program_id(0)
     ext_tiles = own_tiles + 2 * SPT
@@ -62,6 +62,8 @@
                                high_hbm, kext, vext, sems)
         for copy in copies:
             copy.start()
+        q_wide[...] = jnp.zeros_like(q_wide)
+        do_wide[...] = jnp.zeros_like(do_wide)
         dk[...] = jnp.zeros_like(dk)
         dv[...] = jnp.zeros_like(dv)
         for copy in copies:
@@ -74,23 +76,43 @@
                 vt[h][t] = vext[t, :, cols[h]].T
 
     count = cnt_ref[a]
-
-    def score_slot(s, carry):
-        t = idx_ref[a * KSLOT + s]
+    for h in range(heads):
+        for wide, ref in ((q_wide, q_ref), (do_wide, do_ref)):
+            wide[h * TILE:(h + 1) * TILE, cols[h]] = ref[:, cols[h]]
+    split = [slice(h * TILE, (h + 1) * TILE) for h in range(heads)]
+
+    def over_slots(body, carry):
+        def double(i, carry):
+            return body((2 * i, 2 * i + 1), carry)
+
+        def single(s, carry):
+            return body((s,), carry)
+
+        carry = lax.fori_loop(0, count // 2, double, carry)
+        return lax.fori_loop(count // 2 * 2, count, single, carry)
+
+    def tiles(slots):
+        return [idx_ref[a * KSLOT + s] for s in slots]
+
+    def score_slots(slots, carry):
+        blocks = [dot_nt(kext[t], q_wide[...]) for t in tiles(slots)]
         new = []
-        blocks = [dot_nt(kext[t, :, cols[h]], q_ref[:, cols[h]]) for h in range(heads)]
         for h in range(heads):
             old, total = carry[h]
-            top = jnp.maximum(old, jnp.max(fold_rows(blocks[h], jnp.max), axis=0, keepdims=True))
-            weights = jnp.exp2((blocks[h] - top) * EXP2_SCALE)
-            scores[h][s] = weights
-            tops_at[h][s] = top
-            total = total * jnp.exp2((old - top) * EXP2_SCALE) + fold_rows(weights, jnp.sum)
+            parts = [block[:, split[h]] for block in blocks]
+            peak = functools.reduce(jnp.maximum, [fold_rows(part, jnp.max) for part in parts])
+            top = jnp.maximum(old, jnp.max(peak, axis=0, keepdims=True))
+            total = total * jnp.exp2((old - top) * EXP2_SCALE)
+            for s, part in zip(slots, parts):
+                weights = jnp.exp2((part - top) * EXP2_SCALE)
+                scores[h][s] = weights
+                tops_at[h][s] = top
+                total = total + fold_rows(weights, jnp.sum)
             new.append((top, total))
         return tuple(new)
 
     start = (jnp.full((1, TILE), -jnp.inf, jnp.float32), jnp.zeros((8, TILE), jnp.float32))
-    stats = lax.fori_loop(0, count, score_slot, (start,) * heads)
+    stats = over_slots(score_slots, (start,) * heads)
     tops = [top for top, _ in stats]
     inverse = [1.0 / jnp.sum(total, axis=0, keepdims=True) for _, total in stats]
     for h in range(heads):
@@ -101,15 +123,20 @@
         factor = jnp.exp2((tops_at[h][s] - tops[h]) * EXP2_SCALE) * inverse[h]
         return scores[h][s] * factor
 
-    @pl.loop(0, count)
-    def _(s):
-        t = idx_ref[a * KSLOT + s]
-        lows = [weights_of(h, s).astype(jnp.bfloat16) for h in range(heads)]
-        outs = [dot_nn(vt[h][t], lows[h]) for h in range(heads)]
-        terms = [dot_nn(lows[h], do_ref[:, cols[h]]) for h in range(heads)]
+    def joined(blocks, axis):
+        return blocks[0] if len(blocks) == 1 else jnp.concatenate(blocks, axis=axis)
+
+    def value_slots(slots, carry):
+        at = tiles(slots)
+        lows = [[weights_of(h, s).astype(jnp.bfloat16) for h in range(heads)] for s in slots]
+        for t, low in zip(at, lows):
+            dv[t] += dot_nn(joined(low, 1), do_wide[...])
         for h in range(heads):
-            o_acc[h][...] += outs[h]
-        dv[t] += jnp.concatenate(terms, axis=1)
+            o_acc[h][...] += dot_nn(
+                joined([vt[h][t] for t in at], 1), joined([low[h] for low in lows], 0))
+        return carry
+
+    over_slots(value_slots, jnp.int32(0))
 
     deltas = []
     for h in range(heads):
@@ -118,18 +145,24 @@
         deltas.append(jnp.sum(out_t * grads_t, axis=0, keepdims=True))
         o_ref[:, cols[h]] = out_t.T.astype(jnp.bfloat16)
 
-    @pl.loop(0, count)
-    def _(s):
-        t = idx_ref[a * KSLOT + s]
-        grads = [dot_nt(vext[t, :, cols[h]], do_ref[:, cols[h]]) for h in range(heads)]
+    def key_slots(slots, carry):
+        at = tiles(slots)
+        grads = [dot_nt(vext[t], do_wide[...]) for t in at]
         lows = [
-            (weights_of(h, s) * (grads[h] - deltas[h])).astype(jnp.bfloat16) for h in range(heads)
+            [
+                (weights_of(h, s) * (grad[:, split[h]] - deltas[h])).astype(jnp.bfloat16)
+                for h in range(heads)
+            ]
+            for s, grad in zip(slots, grads)
         ]
-        terms = [dot_nn(lows[h], q_ref[:, cols[h]]) for h in range(heads)]
-        query_terms = [dot_nn(kt[h][t], lows[h]) for h in range(heads)]
-        dk[t] += jnp.concatenate(terms, axis=1)
+        for t, low in zip(at, lows):
+            dk[t] += dot_nn(joined(low, 1), q_wide[...])
         for h in range(heads):
-            dq_acc[h][...] += query_terms[h]
+            dq_acc[h][...] += dot_nn(
+                joined([kt[h][t] for t in at], 1), joined([low[h] for low in lows], 0))
+        return carry
+
+    over_slots(key_slots, jnp.int32(0))
 
     for h in range(heads):
         dq_ref[:, cols[h]] = (dq_acc[h][...] * SCALE).T.astype(jnp.bfloat16)
@@ -169,14 +202,13 @@
     width = heads * HD
     col_block = first // heads
     in_block = (first - in_span[0]) // heads
-    out_block = (first - out_span[0]) // heads
     in_width, out_width = in_span[1] * HD, out_span[1] * HD
     smem = pl.BlockSpec(memory_space=pltpu.SMEM)
     hbm = pl.BlockSpec(memory_space=pl.ANY)
     rim = jax.ShapeDtypeStruct((SPT, TILE, 2 * out_width), jnp.bfloat16)
     own = jax.ShapeDtypeStruct((own_tiles, TILE, out_width), jnp.float32)
     out_shape = [
-        jax.ShapeDtypeStruct((rows, out_width), jnp.bfloat16),
+        jax.ShapeDtypeStruct((rows, width), jnp.bfloat16),
         jax.ShapeDtypeStruct((rows, all_cols), jnp.bfloat16),
         own, own, rim, rim,
     ]
@@ -185,7 +217,7 @@
         aliases[8 + len(before)] = 1
         before.append(dq_before)
     if out_before is not None:
-        for at, array in zip((0, 2, 3, 4, 5), out_before):
+        for at, array in zip((2, 3, 4, 5), out_before):
             aliases[8 + len(before)] = at
             before.append(array)
     pairs = own_tiles * 6 * heads
@@ -211,7 +243,7 @@
             hbm, hbm, hbm, hbm,
         ] + [hbm] * len(before),
         out_specs=[
-            pl.BlockSpec((TILE, width), lambda a: (a, out_block)),
+            pl.BlockSpec((TILE, width), lambda a: (a, 0)),
             pl.BlockSpec((TILE, width), lambda a: (a, col_block)),
             hbm, hbm, hbm, hbm,
         ],
@@ -222,6 +254,8 @@
             pltpu.VMEM((ext_tiles, TILE, width), jnp.bfloat16),
             pltpu.VMEM((ext_tiles, TILE, width), jnp.float32),
             pltpu.VMEM((ext_tiles, TILE, width), jnp.float32),
+            pltpu.VMEM((heads * TILE, width), jnp.bfloat16),
+            pltpu.VMEM((heads * TILE, width), jnp.bfloat16),
             pltpu.SemaphoreType.DMA((6,)),
         ] + per_head * heads,
         compiler_params=pltpu.CompilerParams(vmem_limit_bytes=56 * 1024 * 1024),
@@ -231,7 +265,7 @@
             transcendentals=pairs * TILE * TILE,
         ),
     )(idx, cnt, queries, grads, keys, values, low, high, *before)
-    return dq, (out, *rest)
+    return out, dq, rest
 
 
 def finish_kernel(own_tiles, k_own, v_own, ka, va, kb, vb, *refs):
@@ -280,12 +314,8 @@
     return up, [(b, a) for a, b in up]
 
 
-def scatter_heads(block):
-    return lax.all_to_all(block, "head", split_axis=1, concat_axis=0, tiled=True)
-
-
-def gather_heads(block):
-    return lax.all_to_all(block, "head", split_axis=0, concat_axis=1, tiled=True)
+def swap_blocks(blocks):
+    return lax.all_to_all(blocks, "head", split_axis=0, concat_axis=0, tiled=True)
 
 
 def head_plan(heads_here):
@@ -318,35 +348,38 @@
     groups, in_spans, out_spans = head_plan(col_count // HD)
     keys_tiled = key_states.reshape(own_tiles, TILE, col_count)
     values_tiled = value_states.reshape(own_tiles, TILE, col_count)
-    by_head = out_grads.reshape(own_rows, head_devices, col_count)
 
     lows, highs, grads = [], [], []
     for at, heads in in_spans:
         cols = slice(at * HD, (at + heads) * HD)
         packed = jnp.concatenate((keys_tiled[:, :, cols], values_tiled[:, :, cols]), axis=2)
-        grad_part = by_head[:, :, cols]
+        grad_part = jnp.stack([
+            out_grads[:, n * col_count + at * HD:n * col_count + (at + heads) * HD]
+            for n in range(head_devices)
+        ])
         if lows:
             packed, grad_part, lows[-1], highs[-1], grads[-1] = lax.optimization_barrier(
                 (packed, grad_part, lows[-1], highs[-1], grads[-1]))
         lows.append(lax.ppermute(packed[own_tiles - SPT:], "ctx", up))
         highs.append(lax.ppermute(packed[:SPT], "ctx", down))
-        grads.append(scatter_heads(grad_part.reshape(own_rows, -1)))
-
-    dq, parts = None, [None] * len(out_spans)
+        grads.append(swap_blocks(grad_part).reshape(row_count, heads * HD))
+
+    dq, parts, attended = None, [None] * len(out_spans), []
     for at, heads in groups:
         source, target = span_of(at, in_spans), span_of(at, out_spans)
-        dq, parts[target] = attention(
+        out, dq, parts[target] = attention(
             heads, at, in_spans[source], out_spans[target], idx, cnt, queries, grads[source],
             keys_tiled, values_tiled, lows[source], highs[source], dq, parts[target],
         )
-
-    attended, sums = [], ()
-    for span, (out, dk_own, dv_own, low, high) in zip(out_spans, parts):
-        attended.append(gather_heads(out).reshape(own_rows, head_devices, span[1] * HD))
+        attended.append(swap_blocks(out.reshape(head_devices, own_rows, heads * HD)))
+
+    sums = ()
+    for span, (dk_own, dv_own, low, high) in zip(out_spans, parts):
         from_above = lax.ppermute(low, "ctx", down)
         from_below = lax.ppermute(high, "ctx", up)
         sums = finish(span, col_count, dk_own, dv_own, from_above, from_below, sums)
-    attended = jnp.concatenate(attended, axis=2).reshape(own_rows, head_devices * col_count)
+    attended = jnp.concatenate(
+        [part[n] for n in range(head_devices) for part in attended], axis=1)
     return attended, dq, sums[0], sums[1]
 
 

time: 257 us -> 245 us (0.953)
  the two profiles are of different devices: /device:TPU:24 before, /device:TPU:1 now
where the time goes in v3:
time: 245 us; the launch traced here: 249 us
  Pallas kernels  132 us (54%)
  starting transfers between devices  73.7 us (30%)
  local copies, waits for them, and re-layouts  27.2 us (11%)
  waiting for transfers between devices  10.7 us (4%)
  other arithmetic  4.66 us (2%)
    pallas_call x3, Pallas kernels, attention(): pl.pallas_call(functools.partial(attention_kernel, heads, own_tiles, firs...  123 us
    ppermute x2, starting transfers between devices, shards(): from_above = lax.ppermute(low, 'ctx', down)  36 us
    all_to_all x5, starting transfers between devices, swap_blocks(): lax.all_to_all(blocks, 'head', split_axis=0, concat_axis=0, tiled=True)  21.4 us
    unnamed x25, local copies, waits for them, and re-layouts  20.3 us
    pallas_call x2, Pallas kernels, finish(): pl.pallas_call(functools.partial(finish_kernel, own_tiles), grid=(own_til...  8.95 us
    ppermute x2, starting transfers between devices, shards(): lows.append(lax.ppermute(packed[own_tiles - SPT:], 'ctx', up))  6.49 us
    all_to_all x5, waiting for transfers between devices, swap_blocks(): lax.all_to_all(blocks, 'head', split_axis=0, concat_axis=0, tiled=True)  6.18 us
    ppermute x2, starting transfers between devices, shards(): highs.append(lax.ppermute(packed[:SPT], 'ctx', down))  5.94 us
  transfers between devices with their start and end apart: 13, of which 3 were waited for; matrix products, arithmetic and copies ran while one was open for 10% of the time, Pallas kernels for 51%

profile of v3, /device:TPU:1, one launch (start us, length us, event | category | flops | bytes accessed | tf_op | source)
XLA Modules:
  0.0 249.1 jit_solution(8706568010285967246)
XLA Ops:
  0.6 1.2 slice.98
  1.8 0.0 copy-start.4
  1.8 1.3 slice.99
  3.2 1.3 pad_maximum_fusion.2
  4.5 4.6 %collective-permute-start = (bf16[4,384,512]{2,1,0:T(8,128)(2,1)}, bf16[4,384,512]{2,1,0:T(8,128)(2,1)}, u32[]{:S(2)}, u32[]{:S(2)}) collective-permute-start(bf16[4,384,512]{2,1,0:T(8,128)(2,1)} %pad_maximum_fusion.2), channel_id=1, source_target_pairs={{0,4},{4,8},{8,12},{12,16},{16,20},{20,24},{24,28},{1,5},{5,9},{9,... | collective-permute-start | bytes 4718600 | tf_op jit(solution)/shard_map/ppermute | solution.py:363
  9.0 1.9 collective-permute-start.1
  11.0 0.0 copy-done.4
  11.0 0.1 slice_bitcast_fusion.19
  11.0 1.0 pad_maximum_fusion.3
  12.0 4.2 %all-to-all-start = ((bf16[4,384,256]{2,1,0:T(8,128)(2,1)}), bf16[4,384,256]{2,1,0:T(8,128)(2,1)}, u32[]{:S(2)}, u32[]{:S(2)}) async-start(bf16[4,384,256]{2,1,0:T(8,128)(2,1)} %pad_maximum_fusion.3), calls=%async_computation | async-start | bytes 1572864 | tf_op jit(solution)/shard_map/all_to_all | solution.py:318
  16.2 0.0 copy-start.5
  16.3 1.7 slice.96
  17.9 0.5 copy-done.5
  18.4 0.1 slice.97
  18.5 0.1 slice_bitcast_fusion.3
  18.7 1.3 pad_maximum_fusion.1
  20.0 0.4 pad_maximum_fusion
  20.4 6.2 %all-to-all-done = bf16[4,384,256]{2,1,0:T(8,128)(2,1)} async-done(((bf16[4,384,256]{2,1,0:T(8,128)(2,1)}), bf16[4,384,256]{2,1,0:T(8,128)(2,1)}, u32[]{:S(2)}, u32[]{:S(2)}) %all-to-all-start) | async-done | bytes 786464 | tf_op jit(solution)/shard_map/all_to_all | solution.py:318
  26.6 0.1 collective-permute-done.refs_6_
  26.7 4.4 %collective-permute-done.1.refs_7_ = bf16[4,384,512]{2,1,0:T(8,128)(2,1)} collective-permute-done((bf16[4,384,512]{2,1,0:T(8,128)(2,1)}, bf16[4,384,512]{2,1,0:T(8,128)(2,1)}, u32[]{:S(2)}, u32[]{:S(2)}) %collective-permute-start.1) | collective-permute-done | bytes 1572896 | tf_op jit(solution)/shard_map/ppermute | solution.py:364
  31.1 1.9 collective-permute-start.2
  33.0 4.0 %collective-permute-start.3 = (bf16[4,384,1024]{2,1,0:T(8,128)(2,1)S(1)}, bf16[4,384,1024]{2,1,0:T(8,128)(2,1)}, u32[]{:S(2)}, u32[]{:S(2)}) collective-permute-start(bf16[4,384,1024]{2,1,0:T(8,128)(2,1)S(1)} %pad_maximum_fusion), channel_id=1, source_target_pairs={{4,0},{8,4},{12,8},{16,12},{20,16},{24,20},{28,24},{5,1},{9,5},{13... | collective-permute-start | bytes 9437192 | tf_op jit(solution)/shard_map/ppermute | solution.py:364
  37.1 0.6 convert_reduce_fusion
  37.7 0.1 subtract_select_fusion
  37.7 0.1 copy.17
  37.8 0.7 reshape.32.refs_0_
  38.5 4.3 %all-to-all-start.2 = ((bf16[4,384,512]{2,1,0:T(8,128)(2,1)}), bf16[4,384,512]{2,1,0:T(8,128)(2,1)}, u32[]{:S(2)}, u32[]{:S(2)}) async-start(bf16[4,384,512]{2,1,0:T(8,128)(2,1)} %pad_maximum_fusion.1), calls=%async_computation.2 | async-start | bytes 3145728 | tf_op jit(solution)/shard_map/all_to_all | solution.py:318
  42.8 41.0 %shard_map.84 = (bf16[1536,256]{1,0:T(8,128)(2,1)}, bf16[1536,768]{1,0:T(8,128)(2,1)}, f32[4,384,512]{2,1,0:T(8,128)}, f32[4,384,512]{2,1,0:T(8,128)}, bf16[4,38...) custom-call(s32[32]{0:T(128)} %reshape.32.refs_0_, s32[4]{0:T(128)} %get-tuple-element.58.refs_1_, ...), custom_call_target="tpu_custom_call" | custom-call | flops 27179089920 | bytes 11796480 | tf_op jit(solution)/shard_map/pallas_call | solution.py:232
  83.8 0.0 all-to-all-done.2
  83.8 4.4 %all-to-all-start.1 = ((bf16[4,384,256]{2,1,0:T(8,128)(2,1)}), bf16[4,384,256]{2,1,0:T(8,128)(2,1)}, u32[]{:S(2)}, u32[]{:S(2)}) async-start(bf16[4,384,256]{2,1,0:T(8,128)(2,1)} %bitcast.81), calls=%async_computation.1 | async-start | bytes 1572864 | tf_op jit(solution)/shard_map/all_to_all | solution.py:318
  88.2 0.0 collective-permute-done.2.refs_6_
  88.3 0.0 collective-permute-done.3.refs_7_
  88.3 41.0 %shard_map.85 = (bf16[1536,256]{1,0:T(8,128)(2,1)}, bf16[1536,768]{1,0:T(8,128)(2,1)}, f32[4,384,512]{2,1,0:T(8,128)}, f32[4,384,512]{2,1,0:T(8,128)}, bf16[4,38...) custom-call(s32[32]{0:T(128)} %reshape.32.refs_0_, ...), custom_call_target="tpu_custom_call", output_to_operand_aliasing={{1}: (8, {}), {2}: (9, {}), {3}: (10, {}), {4}: (11, {}), {... | custom-call | flops 27179089920 | bytes 11796480 | tf_op jit(solution)/shard_map/pallas_call | solution.py:232
  129.3 21.7 %collective-permute-start.6 = (bf16[4,384,1024]{2,1,0:T(8,128)(2,1)}, bf16[4,384,1024]{2,1,0:T(8,128)(2,1)S(1)}, u32[]{:S(2)}, u32[]{:S(2)}) collective-permute-start(bf16[4,384,1024]{2,1,0:T(8,128)(2,1)} %get-tuple-element.52), channel_id=1, source_target_pairs={{4,0},{8,4},{12,8},{16,12},{20,16},{24,20},{28,24},{5,1},{9,5},{13... | collective-permute-start | bytes 9437192 | tf_op jit(solution)/shard_map/ppermute | solution.py:378
  151.0 1.9 collective-permute-start.7
  153.0 0.0 all-to-all-done.1
  153.0 4.2 %all-to-all-start.3 = ((bf16[4,384,256]{2,1,0:T(8,128)(2,1)}), bf16[4,384,256]{2,1,0:T(8,128)(2,1)}, u32[]{:S(2)}, u32[]{:S(2)}) async-start(bf16[4,384,256]{2,1,0:T(8,128)(2,1)} %bitcast.82), calls=%async_computation.3 | async-start | bytes 1572864 | tf_op jit(solution)/shard_map/all_to_all | solution.py:318
  157.2 41.0 %shard_map.86 = (bf16[1536,256]{1,0:T(8,128)(2,1)}, bf16[1536,768]{1,0:T(8,128)(2,1)}, f32[4,384,256]{2,1,0:T(8,128)}, f32[4,384,256]{2,1,0:T(8,128)}, bf16[4,38...) custom-call(s32[32]{0:T(128)} %reshape.32.refs_0_, ...), custom_call_target="tpu_custom_call", output_to_operand_aliasing={{1}: (8, {})} | custom-call | flops 27179089920 | bytes 11796480 | tf_op jit(solution)/shard_map/pallas_call | solution.py:232
  198.2 0.0 all-to-all-done.3
  198.2 4.2 %all-to-all-start.4 = ((bf16[4,384,256]{2,1,0:T(8,128)(2,1)}), bf16[4,384,256]{2,1,0:T(8,128)(2,1)}, u32[]{:S(2)}, u32[]{:S(2)}) async-start(bf16[4,384,256]{2,1,0:T(8,128)(2,1)} %bitcast.83), calls=%async_computation.4 | async-start | bytes 1572864 | tf_op jit(solution)/shard_map/all_to_all | solution.py:318
  202.4 1.6 fusion.11
  204.0 14.3 %collective-permute-start.4 = (bf16[4,384,512]{2,1,0:T(8,128)(2,1)}, bf16[4,384,512]{2,1,0:T(8,128)(2,1)}, u32[]{:S(2)}, u32[]{:S(2)}) collective-permute-start(bf16[4,384,512]{2,1,0:T(8,128)(2,1)} %get-tuple-element.48), channel_id=1, source_target_pairs={{4,0},{8,4},{12,8},{16,12},{20,16},{24,20},{28,24},{5,1},{9,5},{13... | collective-permute-start | bytes 4718600 | tf_op jit(solution)/shard_map/ppermute | solution.py:378
  218.3 1.9 collective-permute-start.5
  220.3 1.6 fusion.10
  221.9 0.0 all-to-all-done.4
  221.9 1.8 fusion.9
  223.7 1.6 fusion.8
  225.3 1.6 fusion.7
  226.9 1.6 fusion.6
  228.5 1.6 fusion.5
  230.1 1.6 fusion.4
  231.7 1.6 fusion.3
  233.3 1.6 fusion.2
  235.0 1.6 fusion.1
  236.6 1.6 fusion
  238.2 0.0 collective-permute-done.6.ka.va
  238.2 0.0 collective-permute-done.7.kb.vb
  238.2 1.9 copy-done.1
  240.1 4.8 %shard_map.87 = (bf16[1536,768]{1,0:T(8,128)(2,1)}, bf16[1536,768]{1,0:T(8,128)(2,1)}) custom-call(f32[4,384,512]{2,1,0:T(8,128)S(1)} %copy-done, f32[4,384,512]{2,1,0:T(8,128)S(1)} %copy-done.1, bf16[4,384,1024]{2,1,0:T(8,128)(2,1)S(1)} %collective-permute-done.6.ka.va, bf16[4,384,1024]{2,1,0:T(8,128)(2,1)S(1)} %collective-permute-done.6.ka.va, ...), custom_call_target="tpu_custom_call" | custom-call | flops 3145728 | bytes 15728640 | tf_op jit(solution)/shard_map/pallas_call | solution.py:294
  244.9 0.0 collective-permute-done.4.ka.va
  244.9 0.0 collective-permute-done.5.kb.vb
  244.9 0.0 copy-done.2
  245.0 0.0 copy-done.3
  245.0 4.1 %shard_map.88 = (bf16[1536,768]{1,0:T(8,128)(2,1)}, bf16[1536,768]{1,0:T(8,128)(2,1)}) custom-call(f32[4,384,256]{2,1,0:T(8,128)S(1)} %copy-done.2, f32[4,384,256]{2,1,0:T(8,128)S(1)} %copy-done.3, bf16[4,384,512]{2,1,0:T(8,128)(2,1)} %collective-permute-done.4.ka.va, ...), custom_call_target="tpu_custom_call", output_to_operand_aliasing={{0}: (6, {}), {1}: (7, {})} | custom-call | flops 1572864 | bytes 7864320 | tf_op jit(solution)/shard_map/pallas_call | solution.py:294
  (7 shorter events, 0.0 us)
Async XLA Ops:
  1.8 9.2 %copy-start.4 = (bf16[384,3072]{1,0:T(8,128)(2,1)S(1)}, bf16[384,3072]{1,0:T(8,128)(2,1)}, u32[]{:S(2)}) copy-start(bf16[384,3072]{1,0:T(8,128)(2,1)} %param.8) | copy-start | bytes 7077892
  4.5 22.2 %collective-permute-start = (bf16[4,384,512]{2,1,0:T(8,128)(2,1)}, bf16[4,384,512]{2,1,0:T(8,128)(2,1)}, u32[]{:S(2)}, u32[]{:S(2)}) collective-permute-start(bf16[4,384,512]{2,1,0:T(8,128)(2,1)} %pad_maximum_fusion.2), channel_id=1, source_target_pairs={{0,4},{4,8},{8,12},{12,16},{16,20},{20,24},{24,28},{1,5},{5,9},{9,... | collective-permute-start | bytes 4718600 | tf_op jit(solution)/shard_map/ppermute | solution.py:363
  9.0 22.1 %collective-permute-start.1 = (bf16[4,384,512]{2,1,0:T(8,128)(2,1)}, bf16[4,384,512]{2,1,0:T(8,128)(2,1)}, u32[]{:S(2)}, u32[]{:S(2)}) collective-permute-start(bf16[4,384,512]{2,1,0:T(8,128)(2,1)} %pad_maximum_fusion.2), channel_id=1, source_target_pairs={{4,0},{8,4},{12,8},{16,12},{20,16},{24,20},{28,24},{5,1},{9,5},{13... | collective-permute-start | bytes 4718600 | tf_op jit(solution)/shard_map/ppermute | solution.py:364
  12.0 14.5 %all-to-all-start = ((bf16[4,384,256]{2,1,0:T(8,128)(2,1)}), bf16[4,384,256]{2,1,0:T(8,128)(2,1)}, u32[]{:S(2)}, u32[]{:S(2)}) async-start(bf16[4,384,256]{2,1,0:T(8,128)(2,1)} %pad_maximum_fusion.3), calls=%async_computation | async-start | bytes 1572864 | tf_op jit(solution)/shard_map/all_to_all | solution.py:318
  16.2 2.1 copy-start.5
  20.0 17.1 %copy-start.6 = (s32[32,8]{0,1:T(8,128)S(1)}, s32[32,8]{0,1:T(8,128)}, u32[]{:S(2)}) copy-start(s32[32,8]{0,1:T(8,128)} %param.9) | copy-start | bytes 3076
  31.1 57.2 %collective-permute-start.2 = (bf16[4,384,1024]{2,1,0:T(8,128)(2,1)S(1)}, bf16[4,384,1024]{2,1,0:T(8,128)(2,1)}, u32[]{:S(2)}, u32[]{:S(2)}) collective-permute-start(bf16[4,384,1024]{2,1,0:T(8,128)(2,1)S(1)} %pad_maximum_fusion), channel_id=1, source_target_pairs={{0,4},{4,8},{8,12},{12,16},{16,20},{20,24},{24,28},{1,5},{5,9},{9,... | collective-permute-start | bytes 9437192 | tf_op jit(solution)/shard_map/ppermute | solution.py:363
  33.0 55.2 %collective-permute-start.3 = (bf16[4,384,1024]{2,1,0:T(8,128)(2,1)S(1)}, bf16[4,384,1024]{2,1,0:T(8,128)(2,1)}, u32[]{:S(2)}, u32[]{:S(2)}) collective-permute-start(bf16[4,384,1024]{2,1,0:T(8,128)(2,1)S(1)} %pad_maximum_fusion), channel_id=1, source_target_pairs={{4,0},{8,4},{12,8},{16,12},{20,16},{24,20},{28,24},{5,1},{9,5},{13... | collective-permute-start | bytes 9437192 | tf_op jit(solution)/shard_map/ppermute | solution.py:364
  38.5 45.3 %all-to-all-start.2 = ((bf16[4,384,512]{2,1,0:T(8,128)(2,1)}), bf16[4,384,512]{2,1,0:T(8,128)(2,1)}, u32[]{:S(2)}, u32[]{:S(2)}) async-start(bf16[4,384,512]{2,1,0:T(8,128)(2,1)} %pad_maximum_fusion.1), calls=%async_computation.2 | async-start | bytes 3145728 | tf_op jit(solution)/shard_map/all_to_all | solution.py:318
  83.8 69.1 %all-to-all-start.1 = ((bf16[4,384,256]{2,1,0:T(8,128)(2,1)}), bf16[4,384,256]{2,1,0:T(8,128)(2,1)}, u32[]{:S(2)}, u32[]{:S(2)}) async-start(bf16[4,384,256]{2,1,0:T(8,128)(2,1)} %bitcast.81), calls=%async_computation.1 | async-start | bytes 1572864 | tf_op jit(solution)/shard_map/all_to_all | solution.py:318
  129.3 108.9 %collective-permute-start.6 = (bf16[4,384,1024]{2,1,0:T(8,128)(2,1)}, bf16[4,384,1024]{2,1,0:T(8,128)(2,1)S(1)}, u32[]{:S(2)}, u32[]{:S(2)}) collective-permute-start(bf16[4,384,1024]{2,1,0:T(8,128)(2,1)} %get-tuple-element.52), channel_id=1, source_target_pairs={{4,0},{8,4},{12,8},{16,12},{20,16},{24,20},{28,24},{5,1},{9,5},{13... | collective-permute-start | bytes 9437192 | tf_op jit(solution)/shard_map/ppermute | solution.py:378
  151.0 87.2 %collective-permute-start.7 = (bf16[4,384,1024]{2,1,0:T(8,128)(2,1)}, bf16[4,384,1024]{2,1,0:T(8,128)(2,1)}, u32[]{:S(2)}, u32[]{:S(2)}) collective-permute-start(bf16[4,384,1024]{2,1,0:T(8,128)(2,1)} %get-tuple-element.53), channel_id=1, source_target_pairs={{0,4},{4,8},{8,12},{12,16},{16,20},{20,24},{24,28},{1,5},{5,9},{9,... | collective-permute-start | bytes 9437192 | tf_op jit(solution)/shard_map/ppermute | solution.py:379
  153.0 45.2 %all-to-all-start.3 = ((bf16[4,384,256]{2,1,0:T(8,128)(2,1)}), bf16[4,384,256]{2,1,0:T(8,128)(2,1)}, u32[]{:S(2)}, u32[]{:S(2)}) async-start(bf16[4,384,256]{2,1,0:T(8,128)(2,1)} %bitcast.82), calls=%async_computation.3 | async-start | bytes 1572864 | tf_op jit(solution)/shard_map/all_to_all | solution.py:318
  198.2 23.7 %all-to-all-start.4 = ((bf16[4,384,256]{2,1,0:T(8,128)(2,1)}), bf16[4,384,256]{2,1,0:T(8,128)(2,1)}, u32[]{:S(2)}, u32[]{:S(2)}) async-start(bf16[4,384,256]{2,1,0:T(8,128)(2,1)} %bitcast.83), calls=%async_computation.4 | async-start | bytes 1572864 | tf_op jit(solution)/shard_map/all_to_all | solution.py:318
  204.0 40.9 %collective-permute-start.4 = (bf16[4,384,512]{2,1,0:T(8,128)(2,1)}, bf16[4,384,512]{2,1,0:T(8,128)(2,1)}, u32[]{:S(2)}, u32[]{:S(2)}) collective-permute-start(bf16[4,384,512]{2,1,0:T(8,128)(2,1)} %get-tuple-element.48), channel_id=1, source_target_pairs={{4,0},{8,4},{12,8},{16,12},{20,16},{24,20},{28,24},{5,1},{9,5},{13... | collective-permute-start | bytes 4718600 | tf_op jit(solution)/shard_map/ppermute | solution.py:378
  218.3 26.6 %collective-permute-start.5 = (bf16[4,384,512]{2,1,0:T(8,128)(2,1)}, bf16[4,384,512]{2,1,0:T(8,128)(2,1)}, u32[]{:S(2)}, u32[]{:S(2)}) collective-permute-start(bf16[4,384,512]{2,1,0:T(8,128)(2,1)} %get-tuple-element.49), channel_id=1, source_target_pairs={{0,4},{4,8},{8,12},{12,16},{16,20},{20,24},{24,28},{1,5},{5,9},{9,... | collective-permute-start | bytes 4718600 | tf_op jit(solution)/shard_map/ppermute | solution.py:379
  221.9 16.3 %copy-start = (f32[4,384,512]{2,1,0:T(8,128)S(1)}, f32[4,384,512]{2,1,0:T(8,128)}, u32[]{:S(2)}) copy-start(f32[4,384,512]{2,1,0:T(8,128)} %get-tuple-element.50.k_own) | copy-start | bytes 9437188
  238.2 1.9 copy-start.1
  240.1 4.9 %copy-start.2 = (f32[4,384,256]{2,1,0:T(8,128)S(1)}, f32[4,384,256]{2,1,0:T(8,128)}, u32[]{:S(2)}) copy-start(f32[4,384,256]{2,1,0:T(8,128)} %get-tuple-element.46.k_own) | copy-start | bytes 4718596
  240.1 4.9 %copy-start.3 = (f32[4,384,256]{2,1,0:T(8,128)S(1)}, f32[4,384,256]{2,1,0:T(8,128)}, u32[]{:S(2)}) copy-start(f32[4,384,256]{2,1,0:T(8,128)} %get-tuple-element.47.v_own) | copy-start | bytes 4718596
